TPU v7x, 256 devices: a whole 4x4x8 slice. The times are simulated.
256 devices in a mesh: col: 16 (over x_hi, y, core), row: 16 (over z, x_lo).
Axes of the slice: x: 4 (x_hi: 2, x_lo: 2; x = x_hi * 2 + x_lo), y: 4, z: 8, core: 2. Of those that a mesh axis runs over, the one named last changes fastest.
Arguments:
- inverse_root: float32 [4096, 4096], P('row', 'col'), as said below
- factor: float32 [4096, 16384], P('row', 'col'), may hold values from -0.09375 to 0.09375
- structure: int32 [32, 64], P('row', 'col'), may hold values from 0 to 1, as said below
- supernode: int32 [16384], P('col'), may hold values from 0 to 63, as said below
- pivot_inverse: float32 [16384, 1024], P(('col', 'row')), as said below
Outputs:
- offdiag: float32 [4096, 16384], P('row', 'col')
- diag_inverse: float32 [16384, 1024], P(('col', 'row'))
Inputs may be any that keep to these rules, and one draw needn't show every extreme that they name: `inverse_root`: exactly symmetric. A supernode's columns are consecutive, lie within one block of 1024 columns, and number 256 to 1024 in multiples of 256; the numbers in block p start at 4 p and rise by one per supernode. Supernodes of 256 and of 1024 columns occur in every draw. `structure`: equal for all column groups of one supernode. `pivot_inverse`: each block of 1024 rows is symmetric and zero between columns of different supernodes.
All inputs are finite; a program needn't handle non-finite values.
Results may differ from a plain program's by a relative error of at most 0.00007.
Values sent between devices are 32-bit elements; how exact they have to be, the bound alone decides.
No kernel may reach another device: no remote copies, remote signals or barrier semaphores. Data moves between devices by JAX's collectives and lax.ppermute only.
A program may use at most 64 MiB of HBM per device.

v0:
```python
import jax
import jax.numpy as jnp
from jax import lax
from jax.sharding import PartitionSpec as P


def shards(inverse_root, factor, structure, supernode, pivot_inverse):
    rows_local, cols_local = factor.shape
    row_blocks, grains = structure.shape
    block_rows = rows_local // row_blocks
    grain_cols = cols_local // grains
    spread = structure.astype(jnp.float32)[:, None, :, None]
    mask = jnp.broadcast_to(spread, (row_blocks, block_rows, grains, grain_cols)).reshape(
        rows_local, cols_local
    )
    masked = factor * mask
    panel = lax.all_gather(inverse_root, "col", axis=1, tiled=True)
    product = jnp.dot(
        panel,
        lax.all_gather(masked, "row", axis=0, tiled=True),
        precision=lax.Precision.HIGHEST,
        preferred_element_type=jnp.float32,
    )
    offdiag = -product * mask
    local_terms = lax.dot_general(
        masked,
        offdiag,
        (((0,), (0,)), ((), ())),
        precision=lax.Precision.HIGHEST,
        preferred_element_type=jnp.float32,
    )
    same = (supernode[:, None] == supernode[None, :]).astype(jnp.float32)
    shares = lax.psum_scatter(local_terms * same, "row", scatter_dimension=0, tiled=True)
    return (offdiag, pivot_inverse - shares)


def solution(mesh):
    in_specs = (
        P("row", "col"),
        P("row", "col"),
        P("row", "col"),
        P("col"),
        P(("col", "row"), None),
    )
    out_specs = (P("row", "col"), P(("col", "row"), None))
    return jax.shard_map(shards, mesh=mesh, in_specs=in_specs, out_specs=out_specs, check_vma=False)
```

profile of v0, /device:TPU:25, one launch (start us, length us, event | category | flops | bytes accessed | tf_op | source)
XLA Modules:
  0.0 560.8 jit_solution(5660220009521127572)
XLA Ops:
  7.2 0.0 all-gather.5.cloned.1.call-start
  7.2 0.7 all-gather.5.cloned.1.call-update
  7.9 0.0 all-gather.3.cloned.1.call-start
  7.9 0.7 convert_element_type.4
  8.6 0.1 copy.7
  8.7 1.6 copy.8
  10.3 0.3 broadcast_in_dim.2
  10.6 1.1 bitcast_multiply_fusion
  11.7 0.0 all-gather.3.cloned.1.call-update
  11.8 0.0 copy-start
  11.8 0.0 copy-start.2
  11.8 0.0 reduce-scatter.2.cloned.1.call-start
  11.8 61.7 %all-gather.5.cloned.1.call-done = f32[256,4096]{1,0:T(8,128)} async-done(((f32[256,256]{1,0:T(8,128)}), f32[256,4096]{1,0:T(8,128)}) %all-gather.5.cloned.1.call-update) | async-done | bytes 4194320 | tf_op jit(solution)/shard_map/all_gather | solution.py:17
  73.5 352.7 %all-gather.3.cloned.1.call-done = f32[4096,1024]{0,1:T(8,128)} async-done(((f32[256,1024]{0,1:T(8,128)}), f32[4096,1024]{0,1:T(8,128)}) %all-gather.3.cloned.1.call-update) | async-done | bytes 16777232 | tf_op jit(solution)/shard_map/all_gather | solution.py:20
  426.2 16.5 %fusion.1 = f32[256,1024]{0,1:T(8,128)S(1)} fusion(f32[4096,1024]{0,1:T(8,128)} %all-gather.3.cloned.1.call-done, f32[256,4096]{1,0:T(8,128)} %all-gather.5.cloned.1.call-done, f32[128,8,2,128]{3,2,1,0:T(2,128)S(1)} %bitcast.16), kind=kOutput, calls=%fused_computation.3 | convolution fusion | flops 12885426176 | bytes 23068672 | tf_op jit(solution)/shard_map/dot_general | solution.py:18
  442.7 0.0 copy-done
  442.7 0.0 copy-done.2
  442.7 5.1 compare_select_fusion
  447.8 0.0 copy-start.1
  447.8 0.0 reduce-scatter.2.cloned.1.call-update
  447.9 1.3 copy.9
  449.2 103.5 %reduce-scatter.2.cloned.1.call-done = f32[64,1024]{1,0:T(8,128)} async-done(((f32[1024,1024]{1,0:T(8,128)}), f32[64,1024]{1,0:T(8,128)}) %reduce-scatter.2.cloned.1.call-update) | async-done | bytes 262160 | tf_op jit(solution)/shard_map/reduce_scatter | solution.py:33
  552.6 0.0 copy-done.1
  552.6 1.7 sub.3
Async XLA Ops:
  7.2 66.4 %all-gather.5.cloned.1.call-start = ((), (), s32[]{:S(2)}) async-start(), calls=%async_computation.2 | async-start | bytes 4456448 | tf_op jit(solution)/shard_map/all_gather | solution.py:17
  7.9 418.3 %all-gather.3.cloned.1.call-start = ((), (), s32[]{:S(2)}) async-start(), calls=%async_computation.1 | async-start | bytes 17825792 | tf_op jit(solution)/shard_map/all_gather | solution.py:20
  11.8 430.9 %copy-start = (f32[256,1024]{0,1:T(8,128)S(1)}, f32[256,1024]{0,1:T(8,128)}, u32[]{:S(2)}) copy-start(f32[256,1024]{0,1:T(8,128)} %bitcast_multiply_fusion) | copy-start | bytes 3145732
  11.8 430.9 %copy-start.2 = (s32[1024]{0:T(1024)S(1)}, s32[1024]{0:T(1024)}, u32[]{:S(2)}) copy-start(s32[1024]{0:T(1024)} %param.8) | copy-start | bytes 12292
  11.8 540.8 %reduce-scatter.2.cloned.1.call-start = ((), (), s32[]{:S(2)}) async-start(), calls=%async_computation.3 | async-start | bytes 4456448 | tf_op jit(solution)/shard_map/reduce_scatter | solution.py:33
  447.8 104.8 %copy-start.1 = (f32[64,1024]{1,0:T(8,128)S(1)}, f32[64,1024]{1,0:T(8,128)}, u32[]{:S(2)}) copy-start(f32[64,1024]{1,0:T(8,128)} %param.9) | copy-start | bytes 786436
Sparse Core Ops, SparseCore 0:
  10.6 62.9 all-gather.4
  75.9 350.2 all-gather.2
  448.0 104.5 reduce-scatter.1
where the time goes:
time: 564 us; the launch traced here: 561 us
  waiting for transfers between devices  519 us (92%)
  matrix products  21.6 us (4%)
  between operations  13.8 us (2%)
    all_gather x1, waiting for transfers between devices, shards(): lax.all_gather(masked, 'row', axis=0, tiled=True)  353 us
    reduce_scatter x1, waiting for transfers between devices, shards(): lax.psum_scatter(local_terms * same, 'row', scatter_dimension=0, tiled=True)  103 us
    all_gather x1, waiting for transfers between devices, shards(): panel = lax.all_gather(inverse_root, 'col', axis=1, tiled=True)  61.7 us
    dot_general x1, matrix products, shards(): jnp.dot(panel, lax.all_gather(masked, 'row', axis=0, tiled=True), precisi...  16.5 us
  transfers between devices with their start and end apart: 3, of which 3 were waited for; matrix products, arithmetic and copies ran while one was open for 1% of the time, Pallas kernels for 0%

commit v1 on v0

v1 whole, which is shorter than its diff:
```python
import jax
import jax.numpy as jnp
from jax import lax
from jax.experimental import pallas as pl
from jax.experimental.pallas import tpu as pltpu
from jax.sharding import PartitionSpec as P

AXES = ("col", "row")
ROWS = 256
HIGH = lax.Precision.HIGH


def place(index):
    c, r = divmod(index, 16)
    return c >> 3, (c >> 1) & 3, c & 1, r >> 1, r & 1


def index_of(xh, y, core, z, xl):
    return ((xh * 4 + y) * 2 + core) * 16 + z * 2 + xl


def pairs(move, some=lambda xh, y, core, z, xl: True):
    return [(i, index_of(*move(*place(i)))) for i in range(256) if some(*place(i))]


def ring(way):
    return pairs(
        lambda xh, y, core, z, xl: (xh, y, core, (z + (way if core == 0 else -way)) % 8, xl)
    )


def along_plane(k, axis):
    def move(xh, y, core, z, xl):
        if core == axis:
            return xh, (y + k) % 4, core, z, xl
        x = (xh * 2 + xl + k) % 4
        return x >> 1, y, core, z, x & 1

    return pairs(move)


def to_home(way):
    return pairs(
        lambda xh, y, core, z, xl: (xh, y, xl, (z + (way if core == 0 else -way)) % 8, core)
    )


def swap_cores(some=lambda xh, y, core, z, xl: True):
    return pairs(lambda xh, y, core, z, xl: (xh, y, 1 - core, z, xl), some)


def send(value, perm):
    return lax.ppermute(value, AXES, perm)


def dot(a, b):
    return jnp.dot(a, b, precision=HIGH, preferred_element_type=jnp.float32)


TILE = 256


def split(value):
    high = value.astype(jnp.bfloat16)
    return high, (value - high.astype(jnp.float32)).astype(jnp.bfloat16)


def product_kernel(count, at_ref, near_ref, *refs):
    blocks, out_ref, left_high, left_low = refs[:count], *refs[count:]

    @pl.when(pl.program_id(0) == 0)
    def _():
        for b in range(count):
            for s in range(2):
                high, low = split(near_ref[at_ref[2 * b + s]])
                left_high[pl.ds(s * ROWS, ROWS), pl.ds(b * ROWS, ROWS)] = high
                left_low[pl.ds(s * ROWS, ROWS), pl.ds(b * ROWS, ROWS)] = low

    parts = [split(block[...]) for block in blocks]
    high = jnp.concatenate([part[0] for part in parts])
    low = jnp.concatenate([part[1] for part in parts])

    def mul(a, b):
        return jnp.dot(a, b, preferred_element_type=jnp.float32)

    out_ref[...] = (
        mul(left_high[...], low) + mul(left_low[...], high) + mul(left_high[...], high)
    )


def products(at, near, blocks):
    count = len(blocks)
    columns = blocks[0].shape[1]
    return pl.pallas_call(
        lambda *refs: product_kernel(count, *refs),
        grid_spec=pltpu.PrefetchScalarGridSpec(
            num_scalar_prefetch=1,
            grid=(columns // TILE,),
            in_specs=[pl.BlockSpec(near.shape, lambda j, at: (0, 0, 0), pipeline_mode=pl.Buffered(1))]
            + [pl.BlockSpec((ROWS, TILE), lambda j, at: (0, j))] * count,
            out_specs=pl.BlockSpec((2 * ROWS, TILE), lambda j, at: (0, j)),
            scratch_shapes=[pltpu.VMEM((2 * ROWS, count * ROWS), jnp.bfloat16)] * 2,
        ),
        out_shape=jax.ShapeDtypeStruct((2 * ROWS, columns), jnp.float32),
        compiler_params=pltpu.CompilerParams(vmem_limit_bytes=24 * 2**20),
        cost_estimate=pl.CostEstimate(
            flops=6 * 2 * ROWS * count * ROWS * columns,
            bytes_accessed=4 * (near.size + count * ROWS * columns + 2 * ROWS * columns),
            transcendentals=0,
        ),
    )(at, near, *blocks)


def shards(inverse_root, factor, structure, supernode, pivot_inverse):
    col, row = lax.axis_index("col"), lax.axis_index("row")
    core, y, xh = col & 1, (col >> 1) & 3, col >> 3
    xl, z = row & 1, row >> 1
    x = xh * 2 + xl
    never = z < 0
    way = 1 - 2 * core

    def after(value, earlier):
        corner = (1,) * (value.ndim - 2) + (8, 128)
        tile = lax.slice(value, (0,) * value.ndim, corner)
        for array in earlier:
            other = lax.slice(array, (0,) * array.ndim, (1,) * (array.ndim - 2) + (8, 128))
            tile = jnp.where(never, other.reshape(corner), tile)
        return lax.dynamic_update_slice(value, tile, (0,) * value.ndim)

    spread = structure.astype(jnp.float32)[:, None, :, None]
    mask = jnp.broadcast_to(spread, (2, 128, 4, 256)).reshape(256, 1024)
    masked = factor * mask

    own = send(masked, to_home(0))
    block = after(inverse_root, [own])
    around = [send(block, along_plane(-k, 0)) for k in (1, 2, 3)]
    line = jnp.stack([block] + around)
    ahead = [own, after(send(own, ring(1)), around)]
    astern = [own, after(send(own, ring(-1)), around)]
    beside = [send(line, along_plane(-1, 1)), None, send(line, along_plane(-3, 1))]
    ahead.append(after(send(ahead[1], ring(1)), beside[0::2]))
    astern.append(after(send(astern[1], ring(-1)), beside[0::2]))
    beside[1] = send(after(line, beside[0::2]), along_plane(-2, 1))
    ahead.append(after(send(ahead[2], ring(1)), beside[1:2]))
    astern.append(after(send(astern[2], ring(-1)), beside[1:2]))
    near = jnp.concatenate([line] + beside)

    def root_at(zk, s):
        dy = ((zk & 3) - y) & 3
        dx = (((zk & 7) >> 2) * 2 + s - x) & 3
        return jnp.where(core == 0, dx * 4 + dy, dy * 4 + dx)

    last = send(ahead[3][: ROWS // 2], ring(1))
    last_astern = send(astern[3][ROWS // 2 :], ring(-1))
    other = send(after(own, [ahead[3], astern[3]]), swap_cores())
    columns = jnp.where(
        core == 0, jnp.concatenate([own, other]), jnp.concatenate([other, own])
    ).T
    places = [z, z - way, z + way, z - way * 2, z + way * 2, z - way * 3, z + way * 3]
    at = jnp.stack([root_at(zk, s) for zk in places for s in range(2)])
    total = products(
        at.astype(jnp.int32),
        near,
        [own, ahead[1], astern[1], ahead[2], astern[2], ahead[3], astern[3]],
    )
    opposite = jnp.concatenate(
        [
            lax.dynamic_slice(near, (root_at(z + 4, s), 0, 0), (1, ROWS, ROWS))[0]
            for s in range(2)
        ]
    )

    total = total + dot(opposite, jnp.concatenate([last, last_astern]))
    total = total + send(total, swap_cores())

    def term(zk):
        at = (zk & 7) * 128 + core * 64
        return dot(lax.dynamic_slice(columns, (at, 0), (64, 2 * ROWS)), total)

    def step_of(far_sum, near_sum, step):
        arrived = [send(far_sum, ring(1)), send(near_sum, ring(-1))]
        return term(z + way * step) + arrived[0], term(z - way * (step - 1)) + arrived[1]

    far_sum, near_sum = step_of(term(z + way * 4), term(z - way * 3), 3)
    piece = lax.dynamic_slice(total, (core * ROWS, 0), (ROWS, 4 * ROWS))
    out = send(after(piece, [far_sum, near_sum]), to_home(0))
    far_sum, near_sum = step_of(far_sum, near_sum, 2)
    far_sum, near_sum = step_of(far_sum, near_sum, 1)
    far_sum = after(far_sum, [out])
    sums = send(far_sum, to_home(1)) + send(near_sum, to_home(0))

    offdiag = -out * mask
    labels = lax.dynamic_slice(supernode, (row * 64,), (64,))
    same = labels[:, None] == supernode[None, :]
    return offdiag, pivot_inverse + jnp.where(same, sums, 0.0)


def solution(mesh):
    in_specs = (
        P("row", "col"),
        P("row", "col"),
        P("row", "col"),
        P("col"),
        P(("col", "row"), None),
    )
    out_specs = (P("row", "col"), P(("col", "row"), None))
    return jax.shard_map(shards, mesh=mesh, in_specs=in_specs, out_specs=out_specs, check_vma=False)
```

time: 564 us -> 168 us (0.30)
  waiting for transfers between devices: 519 us -> 75.3 us
  starting transfers between devices: 0.12 us -> 53 us
  matrix products: 21.6 us -> 8.18 us
  between operations: 13.8 us -> 1.07 us
  other arithmetic: 3.47 us -> 13.5 us
  Pallas kernels: 0 us -> 8.91 us
    all_gather x2 -> x0, waiting for transfers between devices: 414 us -> none  [the longest x1 353 us: shards(): lax.all_gather(masked, 'row', axis=0, tiled=True)]
    reduce_scatter x1 -> x0, waiting for transfers between devices: 103 us -> none  [shards(): lax.psum_scatter(local_terms * same, 'row', scatter_dimension=0, tiled=True)]
    ppermute x0 -> x26, waiting for transfers between devices: none -> 75.3 us  [send(): return lax.ppermute(value, AXES, perm)]
    ppermute x0 -> x26, starting transfers between devices: none -> 53 us  [send(): return lax.ppermute(value, AXES, perm)]
    dot_general x2 -> x9, matrix products: 21.6 us -> 8.18 us  [dot(): return jnp.dot(a, b, precision=HIGH, preferred_element_type=jnp.float32)]
    pallas_call x0 -> x1, Pallas kernels: none -> 8.91 us  [products(): pl.pallas_call(lambda *refs: product_kernel(count, *refs), grid_spec=pltp...]
  transfers between devices with their start and end apart: 3 -> 26, of which waited for: 3 -> 16; matrix products, arithmetic and copies ran while one was open for 1% -> 11% of each run, Pallas kernels for 0% -> 5%
where the time goes in v1:
time: 168 us; the launch traced here: 166 us
  waiting for transfers between devices  75.3 us (45%)
  starting transfers between devices  53 us (32%)
  other arithmetic  13.5 us (8%)
  Pallas kernels  8.91 us (5%)
  matrix products  8.18 us (5%)
  local copies, waits for them, and re-layouts  6.5 us (4%)
    ppermute x26, waiting for transfers between devices, send(): return lax.ppermute(value, AXES, perm)  75.3 us
    ppermute x26, starting transfers between devices, send(): return lax.ppermute(value, AXES, perm)  53 us
    pallas_call x1, Pallas kernels, products(): pl.pallas_call(lambda *refs: product_kernel(count, *refs), grid_spec=pltp...  8.91 us
    dot_general x9, matrix products, dot(): return jnp.dot(a, b, precision=HIGH, preferred_element_type=jnp.float32)  8.18 us
    unnamed x38, local copies, waits for them, and re-layouts  4.65 us
    dynamic_update_slice x7, other arithmetic, after(): return lax.dynamic_update_slice(value, tile, (0,) * value.ndim)  4.5 us
  transfers between devices with their start and end apart: 26, of which 16 were waited for; matrix products, arithmetic and copies ran while one was open for 11% of the time, Pallas kernels for 5%

profile of v1, /device:TPU:25, one launch (start us, length us, event | category | flops | bytes accessed | tf_op | source)
XLA Modules:
  0.0 166.5 jit_solution(7217884145606681792)
XLA Ops:
  3.0 3.7 %collective-permute-start = (f32[256,1024]{1,0:T(8,128)S(1)}, f32[256,1024]{1,0:T(8,128)S(1)}, u32[]{:S(2)}, u32[]{:S(2)}) collective-permute-start(f32[256,1024]{1,0:T(8,128)S(1)} %mul.211), channel_id=1, source_target_pairs={{0,0},{1,16},{2,2},{3,18},{4,4},{5,20},{6,6},{7,22},{8,8},{9,24},{... | collective-permute-start | bytes 3145736 | tf_op jit(solution)/shard_map/ppermute | solution.py:53
  6.7 12.8 %collective-permute-done.refs_2_ = f32[256,1024]{1,0:T(8,128)S(1)} collective-permute-done((f32[256,1024]{1,0:T(8,128)S(1)}, f32[256,1024]{1,0:T(8,128)S(1)}, u32[]{:S(2)}, u32[]{:S(2)}) %collective-permute-start) | collective-permute-done | bytes 1048608 | tf_op jit(solution)/shard_map/ppermute | solution.py:53
  19.4 1.6 collective-permute-start.8
  21.1 4.0 %collective-permute-start.7 = (f32[256,1024]{1,0:T(8,128)S(1)}, f32[256,1024]{1,0:T(8,128)S(1)}, u32[]{:S(2)}, u32[]{:S(2)}) collective-permute-start(f32[256,1024]{1,0:T(8,128)S(1)} %collective-permute-done.refs_2_), channel_id=1, source_target_pairs={{0,2},{1,3},{2,4},{3,5},{4,6},{5,7},{6,8},{7,9},{8,10},{9,11},{10,... | collective-permute-start | bytes 3145736 | tf_op jit(solution)/shard_map/ppermute | solution.py:53
  25.1 2.8 %collective-permute-start.2 = (f32[256,256]{1,0:T(8,128)S(1)}, f32[256,256]{1,0:T(8,128)S(1)}, u32[]{:S(2)}, u32[]{:S(2)}) collective-permute-start(f32[256,256]{1,0:T(8,128)S(1)} %constant_dynamic-update-slice_fusion.17), channel_id=1, source_target_pairs={{0,64},{1,65},{2,66},{3,67},{4,68},{5,69},{6,70},{7,71},{8,72},{9,... | collective-permute-start | bytes 786440 | tf_op jit(solution)/shard_map/ppermute | solution.py:53
  28.7 1.7 collective-permute-done.1
  30.4 1.6 collective-permute-done.2
  32.0 2.8 %collective-permute-done.3 = f32[256,256]{1,0:T(8,128)S(1)} collective-permute-done((f32[256,256]{1,0:T(8,128)S(1)}, f32[256,256]{1,0:T(8,128)S(1)}, u32[]{:S(2)}, u32[]{:S(2)}) %collective-permute-start.3) | collective-permute-done | bytes 262176 | tf_op jit(solution)/shard_map/ppermute | solution.py:53
  36.3 2.2 %collective-permute-start.5 = (f32[4,256,256]{2,1,0:T(8,128)}, f32[4,256,256]{2,1,0:T(8,128)}, u32[]{:S(2)}, u32[]{:S(2)}) collective-permute-start(f32[4,256,256]{2,1,0:T(8,128)} %pad_maximum_fusion), channel_id=1, source_target_pairs={{0,1},{1,128},{2,3},{3,130},{4,5},{5,132},{6,7},{7,134},{8,9},{9,1... | collective-permute-start | bytes 3145736 | tf_op jit(solution)/shard_map/ppermute | solution.py:53
  40.8 2.7 %collective-permute-start.9 = (f32[256,1024]{1,0:T(8,128)}, f32[256,1024]{1,0:T(8,128)S(1)}, u32[]{:S(2)}, u32[]{:S(2)}) collective-permute-start(f32[256,1024]{1,0:T(8,128)} %copy-done), channel_id=1, source_target_pairs={{0,2},{1,3},{2,4},{3,5},{4,6},{5,7},{6,8},{7,9},{8,10},{9,11},{10,... | collective-permute-start | bytes 3145736 | tf_op jit(solution)/shard_map/ppermute | solution.py:53
  44.7 6.7 %collective-permute-done.4 = f32[4,256,256]{2,1,0:T(8,128)} collective-permute-done((f32[4,256,256]{2,1,0:T(8,128)}, f32[4,256,256]{2,1,0:T(8,128)}, u32[]{:S(2)}, u32[]{:S(2)}) %collective-permute-start.4) | collective-permute-done | bytes 1048608 | tf_op jit(solution)/shard_map/ppermute | solution.py:53
  53.8 7.1 %collective-permute-done.10 = f32[256,1024]{1,0:T(8,128)S(1)} collective-permute-done((f32[256,1024]{1,0:T(8,128)}, f32[256,1024]{1,0:T(8,128)S(1)}, u32[]{:S(2)}, u32[]{:S(2)}) %collective-permute-start.10) | collective-permute-done | bytes 1048608 | tf_op jit(solution)/shard_map/ppermute | solution.py:53
  60.9 2.6 %collective-permute-done.9 = f32[256,1024]{1,0:T(8,128)S(1)} collective-permute-done((f32[256,1024]{1,0:T(8,128)}, f32[256,1024]{1,0:T(8,128)S(1)}, u32[]{:S(2)}, u32[]{:S(2)}) %collective-permute-start.9) | collective-permute-done | bytes 1048608 | tf_op jit(solution)/shard_map/ppermute | solution.py:53
  64.2 3.3 %collective-permute-start.11 = (f32[256,1024]{1,0:T(8,128)S(1)}, f32[256,1024]{1,0:T(8,128)S(1)}, u32[]{:S(2)}, u32[]{:S(2)}) collective-permute-start(f32[256,1024]{1,0:T(8,128)S(1)} %get-tuple-element.8.refs_5_), channel_id=1, source_target_pairs={{0,2},{1,3},{2,4},{3,5},{4,6},{5,7},{6,8},{7,9},{8,10},{9,11},{10,... | collective-permute-start | bytes 3145736 | tf_op jit(solution)/shard_map/ppermute | solution.py:53
  70.4 17.4 %collective-permute-done.11 = f32[256,1024]{1,0:T(8,128)S(1)} collective-permute-done((f32[256,1024]{1,0:T(8,128)S(1)}, f32[256,1024]{1,0:T(8,128)S(1)}, u32[]{:S(2)}, u32[]{:S(2)}) %collective-permute-start.11) | collective-permute-done | bytes 1048608 | tf_op jit(solution)/shard_map/ppermute | solution.py:53
  87.8 4.6 %collective-permute-done.12 = f32[256,1024]{1,0:T(8,128)S(1)} collective-permute-done((f32[256,1024]{1,0:T(8,128)S(1)}, f32[256,1024]{1,0:T(8,128)S(1)}, u32[]{:S(2)}, u32[]{:S(2)}) %collective-permute-start.12) | collective-permute-done | bytes 1048608 | tf_op jit(solution)/shard_map/ppermute | solution.py:53
  94.1 2.7 %collective-permute-start.13 = (f32[128,1024]{1,0:T(8,128)S(1)}, f32[128,1024]{1,0:T(8,128)S(1)}, u32[]{:S(2)}, u32[]{:S(2)}) collective-permute-start(f32[128,1024]{1,0:T(8,128)S(1)} %slice.113), channel_id=1, source_target_pairs={{0,2},{1,3},{2,4},{3,5},{4,6},{5,7},{6,8},{7,9},{8,10},{9,11},{10,... | collective-permute-start | bytes 1572872 | tf_op jit(solution)/shard_map/ppermute | solution.py:53
  96.8 8.9 %shard_map.68 = f32[512,1024]{1,0:T(8,128)S(1)} custom-call(s32[14]{0:T(128)S(1)} %stack.74.refs_0_, f32[16,256,256]{2,1,0:T(8,128)S(1)} %constant_dynamic-update-slice_fusion.refs_1_, f32[256,1024]{1,0:T(8,128)S(1)} %collective-permute-done.refs_2_, f32[256,1024]{1,0:T(8,128)S(1)} %copy-done.1, f32[256,1024]{1,0:T(8,128)} %get-tuple-element.9.refs_4_, ...), custom_call_target="tpu_custom_call" | custom-call | flops 5637144576 | bytes 13631488 | tf_op jit(solution)/shard_map/pallas_call | solution.py:94
  105.9 2.1 %collective-permute-done.13 = f32[128,1024]{1,0:T(8,128)S(1)} collective-permute-done((f32[128,1024]{1,0:T(8,128)S(1)}, f32[128,1024]{1,0:T(8,128)S(1)}, u32[]{:S(2)}, u32[]{:S(2)}) %collective-permute-start.13) | collective-permute-done | bytes 524320 | tf_op jit(solution)/shard_map/ppermute | solution.py:53
  111.1 5.3 %collective-permute-done.16 = f32[256,1024]{1,0:T(8,128)} collective-permute-done((f32[256,1024]{1,0:T(8,128)}, f32[256,1024]{1,0:T(8,128)}, u32[]{:S(2)}, u32[]{:S(2)}) %collective-permute-start.16) | collective-permute-done | bytes 1048608 | tf_op jit(solution)/shard_map/ppermute | solution.py:53
  116.5 1.8 %maximum_select_fusion = f32[512,1024]{1,0:T(8,128)S(1)} fusion(f32[256,1024]{1,0:T(8,128)} %collective-permute-done.16, f32[256,1024]{1,0:T(8,128)S(1)} %collective-permute-done.refs_2_, pred[]{:T(512)S(6)} %eq.8), kind=kLoop, calls=%fused_computation | loop fusion | flops 1572864 | bytes 4194305 | tf_op jit(solution)/shard_map/jit(_where)/select_n | solution.py:156
  118.3 2.8 %add.280 = f32[512,1024]{1,0:T(8,128)S(1)} add(f32[512,1024]{1,0:T(8,128)} %copy-done.4, f32[512,1024]{1,0:T(8,128)} %collective-permute-done.15) | non-fusion elementwise | flops 524288 | bytes 6291456 | tf_op jit(solution)/shard_map/add | solution.py:174
  125.8 2.7 %collective-permute-done.17 = f32[64,1024]{1,0:T(8,128)S(1)} collective-permute-done((f32[64,1024]{1,0:T(8,128)S(1)}, f32[64,1024]{1,0:T(8,128)S(1)}, u32[]{:S(2)}, u32[]{:S(2)}) %collective-permute-start.17) | collective-permute-done | bytes 262176 | tf_op jit(solution)/shard_map/ppermute | solution.py:53
  129.4 2.4 %collective-permute-start.23 = (f32[64,1024]{1,0:T(8,128)S(1)}, f32[64,1024]{1,0:T(8,128)S(1)}, u32[]{:S(2)}, u32[]{:S(2)}) collective-permute-start(f32[64,1024]{1,0:T(8,128)S(1)} %convolution_add_fusion.5), channel_id=1, source_target_pairs={{0,14},{1,15},{2,0},{3,1},{4,2},{5,3},{6,4},{7,5},{8,6},{9,7},{10,... | collective-permute-start | bytes 786440 | tf_op jit(solution)/shard_map/ppermute | solution.py:53
  132.7 2.2 %collective-permute-start.20 = (f32[64,1024]{1,0:T(8,128)S(1)}, f32[64,1024]{1,0:T(8,128)S(1)}, u32[]{:S(2)}, u32[]{:S(2)}) collective-permute-start(f32[64,1024]{1,0:T(8,128)S(1)} %convolution_add_fusion.4), channel_id=1, source_target_pairs={{0,2},{1,3},{2,4},{3,5},{4,6},{5,7},{6,8},{7,9},{8,10},{9,11},{10,... | collective-permute-start | bytes 786440 | tf_op jit(solution)/shard_map/ppermute | solution.py:53
  134.9 6.5 %collective-permute-start.19 = (f32[256,1024]{1,0:T(8,128)S(1)}, f32[256,1024]{1,0:T(8,128)S(1)}, u32[]{:S(2)}, u32[]{:S(2)}) collective-permute-start(f32[256,1024]{1,0:T(8,128)S(1)} %constant_dynamic-update-slice_fusion.8), channel_id=1, source_target_pairs={{0,0},{1,16},{2,2},{3,18},{4,4},{5,20},{6,6},{7,22},{8,8},{9,24},{... | collective-permute-start | bytes 3145736 | tf_op jit(solution)/shard_map/ppermute | solution.py:53
  143.3 2.7 %collective-permute-start.21 = (f32[64,1024]{1,0:T(8,128)S(1)}, f32[64,1024]{1,0:T(8,128)S(1)}, u32[]{:S(2)}, u32[]{:S(2)}) collective-permute-start(f32[64,1024]{1,0:T(8,128)S(1)} %convolution_add_fusion.2), channel_id=1, source_target_pairs={{0,2},{1,3},{2,4},{3,5},{4,6},{5,7},{6,8},{7,9},{8,10},{9,11},{10,... | collective-permute-start | bytes 786440 | tf_op jit(solution)/shard_map/ppermute | solution.py:53
  146.1 2.8 %collective-permute-done.24 = f32[64,1024]{1,0:T(8,128)S(1)} collective-permute-done((f32[64,1024]{1,0:T(8,128)S(1)}, f32[64,1024]{1,0:T(8,128)S(1)}, u32[]{:S(2)}, u32[]{:S(2)}) %collective-permute-start.24) | collective-permute-done | bytes 262176 | tf_op jit(solution)/shard_map/ppermute | solution.py:53
  149.8 7.0 %collective-permute-start.25 = (f32[64,1024]{1,0:T(8,128)S(1)}, f32[64,1024]{1,0:T(8,128)S(1)}, u32[]{:S(2)}, u32[]{:S(2)}) collective-permute-start(f32[64,1024]{1,0:T(8,128)S(1)} %convolution_add_fusion.1), channel_id=1, source_target_pairs={{0,0},{1,16},{2,2},{3,18},{4,4},{5,20},{6,6},{7,22},{8,8},{9,24},{... | collective-permute-start | bytes 786440 | tf_op jit(solution)/shard_map/ppermute | solution.py:53
  157.7 1.8 %collective-permute-start.22 = (f32[64,1024]{1,0:T(8,128)S(1)}, f32[64,1024]{1,0:T(8,128)S(1)}, u32[]{:S(2)}, u32[]{:S(2)}) collective-permute-start(f32[64,1024]{1,0:T(8,128)S(1)} %constant_dynamic-update-slice_fusion.7), channel_id=1, source_target_pairs={{0,2},{1,18},{2,4},{3,20},{4,6},{5,22},{6,8},{7,24},{8,10},{9,26},... | collective-permute-start | bytes 786440 | tf_op jit(solution)/shard_map/ppermute | solution.py:53
  160.6 2.2 %collective-permute-done.25 = f32[64,1024]{1,0:T(8,128)S(1)} collective-permute-done((f32[64,1024]{1,0:T(8,128)S(1)}, f32[64,1024]{1,0:T(8,128)S(1)}, u32[]{:S(2)}, u32[]{:S(2)}) %collective-permute-start.25) | collective-permute-done | bytes 262176 | tf_op jit(solution)/shard_map/ppermute | solution.py:53
  162.8 2.8 %collective-permute-done.22 = f32[64,1024]{1,0:T(8,128)S(1)} collective-permute-done((f32[64,1024]{1,0:T(8,128)S(1)}, f32[64,1024]{1,0:T(8,128)S(1)}, u32[]{:S(2)}, u32[]{:S(2)}) %collective-permute-start.22) | collective-permute-done | bytes 262176 | tf_op jit(solution)/shard_map/ppermute | solution.py:53
  (91 shorter events, 31.2 us)
Async XLA Ops:
  1.8 23.3 %copy-start.5 = (f32[256,256]{1,0:T(8,128)S(1)}, f32[256,256]{1,0:T(8,128)}, u32[]{:S(2)}) copy-start(f32[256,256]{1,0:T(8,128)} %param.5) | copy-start | bytes 786436
  3.0 16.5 %collective-permute-start = (f32[256,1024]{1,0:T(8,128)S(1)}, f32[256,1024]{1,0:T(8,128)S(1)}, u32[]{:S(2)}, u32[]{:S(2)}) collective-permute-start(f32[256,1024]{1,0:T(8,128)S(1)} %mul.211), channel_id=1, source_target_pairs={{0,0},{1,16},{2,2},{3,18},{4,4},{5,20},{6,6},{7,22},{8,8},{9,24},{... | collective-permute-start | bytes 3145736 | tf_op jit(solution)/shard_map/ppermute | solution.py:53
  19.4 19.1 %collective-permute-start.8 = (f32[256,1024]{1,0:T(8,128)S(1)}, f32[256,1024]{1,0:T(8,128)}, u32[]{:S(2)}, u32[]{:S(2)}) collective-permute-start(f32[256,1024]{1,0:T(8,128)S(1)} %collective-permute-done.refs_2_), channel_id=1, source_target_pairs={{0,14},{1,15},{2,0},{3,1},{4,2},{5,3},{6,4},{7,5},{8,6},{9,7},{10,... | collective-permute-start | bytes 3145736 | tf_op jit(solution)/shard_map/ppermute | solution.py:53
  21.1 17.5 %collective-permute-start.7 = (f32[256,1024]{1,0:T(8,128)S(1)}, f32[256,1024]{1,0:T(8,128)S(1)}, u32[]{:S(2)}, u32[]{:S(2)}) collective-permute-start(f32[256,1024]{1,0:T(8,128)S(1)} %collective-permute-done.refs_2_), channel_id=1, source_target_pairs={{0,2},{1,3},{2,4},{3,5},{4,6},{5,7},{6,8},{7,9},{8,10},{9,11},{10,... | collective-permute-start | bytes 3145736 | tf_op jit(solution)/shard_map/ppermute | solution.py:53
  25.1 5.2 %collective-permute-start.1 = (f32[256,256]{1,0:T(8,128)S(1)}, f32[256,256]{1,0:T(8,128)S(1)}, u32[]{:S(2)}, u32[]{:S(2)}) collective-permute-start(f32[256,256]{1,0:T(8,128)S(1)} %constant_dynamic-update-slice_fusion.17), channel_id=1, source_target_pairs={{0,96},{1,97},{2,98},{3,99},{4,100},{5,101},{6,102},{7,103},{8,104... | collective-permute-start | bytes 786440 | tf_op jit(solution)/shard_map/ppermute | solution.py:53
  25.1 6.9 %collective-permute-start.2 = (f32[256,256]{1,0:T(8,128)S(1)}, f32[256,256]{1,0:T(8,128)S(1)}, u32[]{:S(2)}, u32[]{:S(2)}) collective-permute-start(f32[256,256]{1,0:T(8,128)S(1)} %constant_dynamic-update-slice_fusion.17), channel_id=1, source_target_pairs={{0,64},{1,65},{2,66},{3,67},{4,68},{5,69},{6,70},{7,71},{8,72},{9,... | collective-permute-start | bytes 786440 | tf_op jit(solution)/shard_map/ppermute | solution.py:53
  27.9 6.8 %collective-permute-start.3 = (f32[256,256]{1,0:T(8,128)S(1)}, f32[256,256]{1,0:T(8,128)S(1)}, u32[]{:S(2)}, u32[]{:S(2)}) collective-permute-start(f32[256,256]{1,0:T(8,128)S(1)} %constant_dynamic-update-slice_fusion.17), channel_id=1, source_target_pairs={{0,32},{1,33},{2,34},{3,35},{4,36},{5,37},{6,38},{7,39},{8,40},{9,... | collective-permute-start | bytes 786440 | tf_op jit(solution)/shard_map/ppermute | solution.py:53
  30.4 10.4 %copy-start.6 = (f32[256,256]{1,0:T(8,128)}, f32[256,256]{1,0:T(8,128)S(1)}, u32[]{:S(2)}) copy-start(f32[256,256]{1,0:T(8,128)S(1)} %collective-permute-done.1) | copy-start | bytes 786436
  35.9 15.5 %collective-permute-start.4 = (f32[4,256,256]{2,1,0:T(8,128)}, f32[4,256,256]{2,1,0:T(8,128)}, u32[]{:S(2)}, u32[]{:S(2)}) collective-permute-start(f32[4,256,256]{2,1,0:T(8,128)} %pad_maximum_fusion), channel_id=1, source_target_pairs={{0,129},{1,0},{2,131},{3,2},{4,133},{5,4},{6,135},{7,6},{8,137},{9... | collective-permute-start | bytes 3145736 | tf_op jit(solution)/shard_map/ppermute | solution.py:53
  36.3 15.0 %collective-permute-start.5 = (f32[4,256,256]{2,1,0:T(8,128)}, f32[4,256,256]{2,1,0:T(8,128)}, u32[]{:S(2)}, u32[]{:S(2)}) collective-permute-start(f32[4,256,256]{2,1,0:T(8,128)} %pad_maximum_fusion), channel_id=1, source_target_pairs={{0,1},{1,128},{2,3},{3,130},{4,5},{5,132},{6,7},{7,134},{8,9},{9,1... | collective-permute-start | bytes 3145736 | tf_op jit(solution)/shard_map/ppermute | solution.py:53
  40.8 20.1 %collective-permute-start.10 = (f32[256,1024]{1,0:T(8,128)}, f32[256,1024]{1,0:T(8,128)S(1)}, u32[]{:S(2)}, u32[]{:S(2)}) collective-permute-start(f32[256,1024]{1,0:T(8,128)} %get-tuple-element.9.refs_4_), channel_id=1, source_target_pairs={{0,14},{1,15},{2,0},{3,1},{4,2},{5,3},{6,4},{7,5},{8,6},{9,7},{10,... | collective-permute-start | bytes 3145736 | tf_op jit(solution)/shard_map/ppermute | solution.py:53
  40.8 22.7 %collective-permute-start.9 = (f32[256,1024]{1,0:T(8,128)}, f32[256,1024]{1,0:T(8,128)S(1)}, u32[]{:S(2)}, u32[]{:S(2)}) collective-permute-start(f32[256,1024]{1,0:T(8,128)} %copy-done), channel_id=1, source_target_pairs={{0,2},{1,3},{2,4},{3,5},{4,6},{5,7},{6,8},{7,9},{8,10},{9,11},{10,... | collective-permute-start | bytes 3145736 | tf_op jit(solution)/shard_map/ppermute | solution.py:53
  43.6 23.9 %copy-start.7 = (f32[256,256]{1,0:T(8,128)S(1)}, f32[256,256]{1,0:T(8,128)}, u32[]{:S(2)}) copy-start(f32[256,256]{1,0:T(8,128)} %copy-done.6) | copy-start | bytes 786436
  43.6 23.9 %copy-start.9 = (f32[256,256]{1,0:T(8,128)S(1)}, f32[256,256]{1,0:T(8,128)}, u32[]{:S(2)}) copy-start(f32[256,256]{1,0:T(8,128)} %copy-done.8) | copy-start | bytes 786436
  43.6 23.9 %copy-start.11 = (f32[256,256]{1,0:T(8,128)S(1)}, f32[256,256]{1,0:T(8,128)}, u32[]{:S(2)}) copy-start(f32[256,256]{1,0:T(8,128)} %copy-done.10) | copy-start | bytes 786436
  52.6 16.3 %collective-permute-start.6 = (f32[4,256,256]{2,1,0:T(8,128)}, f32[4,256,256]{2,1,0:T(8,128)S(1)}, u32[]{:S(2)}, u32[]{:S(2)}) collective-permute-start(f32[4,256,256]{2,1,0:T(8,128)} %constant_dynamic-update-slice_fusion.16), channel_id=1, source_target_pairs={{0,128},{1,129},{2,130},{3,131},{4,132},{5,133},{6,134},{7,135},{8... | collective-permute-start | bytes 3145736 | tf_op jit(solution)/shard_map/ppermute | solution.py:53
  64.2 23.6 %collective-permute-start.11 = (f32[256,1024]{1,0:T(8,128)S(1)}, f32[256,1024]{1,0:T(8,128)S(1)}, u32[]{:S(2)}, u32[]{:S(2)}) collective-permute-start(f32[256,1024]{1,0:T(8,128)S(1)} %get-tuple-element.8.refs_5_), channel_id=1, source_target_pairs={{0,2},{1,3},{2,4},{3,5},{4,6},{5,7},{6,8},{7,9},{8,10},{9,11},{10,... | collective-permute-start | bytes 3145736 | tf_op jit(solution)/shard_map/ppermute | solution.py:53
  67.5 24.9 %collective-permute-start.12 = (f32[256,1024]{1,0:T(8,128)S(1)}, f32[256,1024]{1,0:T(8,128)S(1)}, u32[]{:S(2)}, u32[]{:S(2)}) collective-permute-start(f32[256,1024]{1,0:T(8,128)S(1)} %get-tuple-element.7.refs_6_), channel_id=1, source_target_pairs={{0,14},{1,15},{2,0},{3,1},{4,2},{5,3},{6,4},{7,5},{8,6},{9,7},{10,... | collective-permute-start | bytes 3145736 | tf_op jit(solution)/shard_map/ppermute | solution.py:53
  70.3 26.5 %copy-start.1 = (f32[256,1024]{1,0:T(8,128)S(1)}, f32[256,1024]{1,0:T(8,128)}, u32[]{:S(2)}) copy-start(f32[256,1024]{1,0:T(8,128)} %copy-done) | copy-start | bytes 3145732
  93.7 12.2 %collective-permute-start.14 = (f32[128,1024]{1,0:T(8,128)S(1)}, f32[128,1024]{1,0:T(8,128)S(1)}, u32[]{:S(2)}, u32[]{:S(2)}) collective-permute-start(f32[128,1024]{1,0:T(8,128)S(1)} %slice.114), channel_id=1, source_target_pairs={{0,14},{1,15},{2,0},{3,1},{4,2},{5,3},{6,4},{7,5},{8,6},{9,7},{10,... | collective-permute-start | bytes 1572872 | tf_op jit(solution)/shard_map/ppermute | solution.py:53
  94.1 13.9 %collective-permute-start.13 = (f32[128,1024]{1,0:T(8,128)S(1)}, f32[128,1024]{1,0:T(8,128)S(1)}, u32[]{:S(2)}, u32[]{:S(2)}) collective-permute-start(f32[128,1024]{1,0:T(8,128)S(1)} %slice.113), channel_id=1, source_target_pairs={{0,2},{1,3},{2,4},{3,5},{4,6},{5,7},{6,8},{7,9},{8,10},{9,11},{10,... | collective-permute-start | bytes 1572872 | tf_op jit(solution)/shard_map/ppermute | solution.py:53
  109.4 8.9 %collective-permute-start.15 = (f32[512,1024]{1,0:T(8,128)S(1)}, f32[512,1024]{1,0:T(8,128)}, u32[]{:S(2)}, u32[]{:S(2)}) collective-permute-start(f32[512,1024]{1,0:T(8,128)S(1)} %add.279), channel_id=1, source_target_pairs={{0,16},{1,17},{2,18},{3,19},{4,20},{5,21},{6,22},{7,23},{8,24},{9,... | collective-permute-start | bytes 6291464 | tf_op jit(solution)/shard_map/ppermute | solution.py:53
  111.0 5.5 %collective-permute-start.16 = (f32[256,1024]{1,0:T(8,128)}, f32[256,1024]{1,0:T(8,128)}, u32[]{:S(2)}, u32[]{:S(2)}) collective-permute-start(f32[256,1024]{1,0:T(8,128)} %get-tuple-element.4), channel_id=1, source_target_pairs={{0,16},{1,17},{2,18},{3,19},{4,20},{5,21},{6,22},{7,23},{8,24},{9,... | collective-permute-start | bytes 3145736 | tf_op jit(solution)/shard_map/ppermute | solution.py:53
  122.0 6.5 %collective-permute-start.17 = (f32[64,1024]{1,0:T(8,128)S(1)}, f32[64,1024]{1,0:T(8,128)S(1)}, u32[]{:S(2)}, u32[]{:S(2)}) collective-permute-start(f32[64,1024]{1,0:T(8,128)S(1)} %fusion.14), channel_id=1, source_target_pairs={{0,14},{1,15},{2,0},{3,1},{4,2},{5,3},{6,4},{7,5},{8,6},{9,7},{10,... | collective-permute-start | bytes 786440 | tf_op jit(solution)/shard_map/ppermute | solution.py:53
  124.3 7.6 %collective-permute-start.18 = (f32[64,1024]{1,0:T(8,128)S(1)}, f32[64,1024]{1,0:T(8,128)S(1)}, u32[]{:S(2)}, u32[]{:S(2)}) collective-permute-start(f32[64,1024]{1,0:T(8,128)S(1)} %fusion.11), channel_id=1, source_target_pairs={{0,2},{1,3},{2,4},{3,5},{4,6},{5,7},{6,8},{7,9},{8,10},{9,11},{10,... | collective-permute-start | bytes 786440 | tf_op jit(solution)/shard_map/ppermute | solution.py:53
  129.4 12.0 %collective-permute-start.23 = (f32[64,1024]{1,0:T(8,128)S(1)}, f32[64,1024]{1,0:T(8,128)S(1)}, u32[]{:S(2)}, u32[]{:S(2)}) collective-permute-start(f32[64,1024]{1,0:T(8,128)S(1)} %convolution_add_fusion.5), channel_id=1, source_target_pairs={{0,14},{1,15},{2,0},{3,1},{4,2},{5,3},{6,4},{7,5},{8,6},{9,7},{10,... | collective-permute-start | bytes 786440 | tf_op jit(solution)/shard_map/ppermute | solution.py:53
  132.7 9.7 %collective-permute-start.20 = (f32[64,1024]{1,0:T(8,128)S(1)}, f32[64,1024]{1,0:T(8,128)S(1)}, u32[]{:S(2)}, u32[]{:S(2)}) collective-permute-start(f32[64,1024]{1,0:T(8,128)S(1)} %convolution_add_fusion.4), channel_id=1, source_target_pairs={{0,2},{1,3},{2,4},{3,5},{4,6},{5,7},{6,8},{7,9},{8,10},{9,11},{10,... | collective-permute-start | bytes 786440 | tf_op jit(solution)/shard_map/ppermute | solution.py:53
  134.9 22.7 %collective-permute-start.19 = (f32[256,1024]{1,0:T(8,128)S(1)}, f32[256,1024]{1,0:T(8,128)S(1)}, u32[]{:S(2)}, u32[]{:S(2)}) collective-permute-start(f32[256,1024]{1,0:T(8,128)S(1)} %constant_dynamic-update-slice_fusion.8), channel_id=1, source_target_pairs={{0,0},{1,16},{2,2},{3,18},{4,4},{5,20},{6,6},{7,22},{8,8},{9,24},{... | collective-permute-start | bytes 3145736 | tf_op jit(solution)/shard_map/ppermute | solution.py:53
  142.3 6.5 %collective-permute-start.24 = (f32[64,1024]{1,0:T(8,128)S(1)}, f32[64,1024]{1,0:T(8,128)S(1)}, u32[]{:S(2)}, u32[]{:S(2)}) collective-permute-start(f32[64,1024]{1,0:T(8,128)S(1)} %convolution_add_fusion), channel_id=1, source_target_pairs={{0,14},{1,15},{2,0},{3,1},{4,2},{5,3},{6,4},{7,5},{8,6},{9,7},{10,... | collective-permute-start | bytes 786440 | tf_op jit(solution)/shard_map/ppermute | solution.py:53
  143.3 13.4 %collective-permute-start.21 = (f32[64,1024]{1,0:T(8,128)S(1)}, f32[64,1024]{1,0:T(8,128)S(1)}, u32[]{:S(2)}, u32[]{:S(2)}) collective-permute-start(f32[64,1024]{1,0:T(8,128)S(1)} %convolution_add_fusion.2), channel_id=1, source_target_pairs={{0,2},{1,3},{2,4},{3,5},{4,6},{5,7},{6,8},{7,9},{8,10},{9,11},{10,... | collective-permute-start | bytes 786440 | tf_op jit(solution)/shard_map/ppermute | solution.py:53
  149.8 13.1 %collective-permute-start.25 = (f32[64,1024]{1,0:T(8,128)S(1)}, f32[64,1024]{1,0:T(8,128)S(1)}, u32[]{:S(2)}, u32[]{:S(2)}) collective-permute-start(f32[64,1024]{1,0:T(8,128)S(1)} %convolution_add_fusion.1), channel_id=1, source_target_pairs={{0,0},{1,16},{2,2},{3,18},{4,4},{5,20},{6,6},{7,22},{8,8},{9,24},{... | collective-permute-start | bytes 786440 | tf_op jit(solution)/shard_map/ppermute | solution.py:53
  157.7 8.0 %collective-permute-start.22 = (f32[64,1024]{1,0:T(8,128)S(1)}, f32[64,1024]{1,0:T(8,128)S(1)}, u32[]{:S(2)}, u32[]{:S(2)}) collective-permute-start(f32[64,1024]{1,0:T(8,128)S(1)} %constant_dynamic-update-slice_fusion.7), channel_id=1, source_target_pairs={{0,2},{1,18},{2,4},{3,20},{4,6},{5,22},{6,8},{7,24},{8,10},{9,26},... | collective-permute-start | bytes 786440 | tf_op jit(solution)/shard_map/ppermute | solution.py:53
  (9 other events, 47.7 us)

commit v2 on v1

--- a/solution.py
+++ b/solution.py
@@ -136,13 +136,14 @@
     around = [send(block, along_plane(-k, 0)) for k in (1, 2, 3)]
     line = jnp.stack([block] + around)
     ahead = [own, after(send(own, ring(1)), around)]
-    astern = [own, after(send(own, ring(-1)), around)]
+    astern = [own, send(own, ring(-1))]
     beside = [send(line, along_plane(-1, 1)), None, send(line, along_plane(-3, 1))]
-    ahead.append(after(send(ahead[1], ring(1)), beside[0::2]))
-    astern.append(after(send(astern[1], ring(-1)), beside[0::2]))
+    other = send(own, swap_cores())
+    ahead.append(after(send(ahead[1], ring(1)), beside[0::2] + [other]))
+    astern.append(send(astern[1], ring(-1)))
     beside[1] = send(after(line, beside[0::2]), along_plane(-2, 1))
     ahead.append(after(send(ahead[2], ring(1)), beside[1:2]))
-    astern.append(after(send(astern[2], ring(-1)), beside[1:2]))
+    astern.append(send(astern[2], ring(-1)))
     near = jnp.concatenate([line] + beside)
 
     def root_at(zk, s):
@@ -152,7 +153,6 @@
 
     last = send(ahead[3][: ROWS // 2], ring(1))
     last_astern = send(astern[3][ROWS // 2 :], ring(-1))
-    other = send(after(own, [ahead[3], astern[3]]), swap_cores())
     columns = jnp.where(
         core == 0, jnp.concatenate([own, other]), jnp.concatenate([other, own])
     ).T

time: 168 us -> 159 us (0.946)
  other arithmetic: 13.5 us -> 10.1 us
  waiting for transfers between devices: 75.3 us -> 72.3 us
  starting transfers between devices: 53 us -> 50.7 us
    ppermute x26, waiting for transfers between devices: 75.3 us -> 72.3 us  [send(): return lax.ppermute(value, AXES, perm)]
    dynamic_update_slice x7, other arithmetic: 4.5 us -> 1.99 us  [after(): return lax.dynamic_update_slice(value, tile, (0,) * value.ndim)]
    ppermute x26, starting transfers between devices: 53 us -> 50.7 us  [send(): return lax.ppermute(value, AXES, perm)]
    unnamed x38 -> x25, local copies, waits for them, and re-layouts: 4.65 us -> 4.55 us
  transfers between devices with their start and end apart: 26 -> 26, of which waited for: 16 -> 15; matrix products, arithmetic and copies ran while one was open for 11% -> 12% of each run, Pallas kernels for 5% -> 6%
where the time goes in v2:
time: 159 us; the launch traced here: 158 us
  waiting for transfers between devices  72.3 us (45%)
  starting transfers between devices  50.7 us (32%)
  other arithmetic  10.1 us (6%)
  Pallas kernels  8.98 us (6%)
  matrix products  8.86 us (6%)
  local copies, waits for them, and re-layouts  6.44 us (4%)
    ppermute x26, waiting for transfers between devices, send(): return lax.ppermute(value, AXES, perm)  72.3 us
    ppermute x26, starting transfers between devices, send(): return lax.ppermute(value, AXES, perm)  50.7 us
    pallas_call x1, Pallas kernels, products(): pl.pallas_call(lambda *refs: product_kernel(count, *refs), grid_spec=pltp...  8.98 us
    dot_general x9, matrix products, dot(): return jnp.dot(a, b, precision=HIGH, preferred_element_type=jnp.float32)  8.86 us
    unnamed x25, local copies, waits for them, and re-layouts  4.55 us
  transfers between devices with their start and end apart: 26, of which 15 were waited for; matrix products, arithmetic and copies ran while one was open for 12% of the time, Pallas kernels for 6%

profile of v2, /device:TPU:25, one launch (start us, length us, event | category | flops | bytes accessed | tf_op | source)
XLA Modules:
  0.0 158.4 jit_solution(10347087624103163696)
XLA Ops:
  2.1 3.8 %collective-permute-start = (f32[256,1024]{1,0:T(8,128)S(1)}, f32[256,1024]{1,0:T(8,128)S(1)}, u32[]{:S(2)}, u32[]{:S(2)}) collective-permute-start(f32[256,1024]{1,0:T(8,128)S(1)} %mul.211), channel_id=1, source_target_pairs={{0,0},{1,16},{2,2},{3,18},{4,4},{5,20},{6,6},{7,22},{8,8},{9,24},{... | collective-permute-start | bytes 3145736 | tf_op jit(solution)/shard_map/ppermute | solution.py:53
  5.9 12.9 %collective-permute-done.refs_2_ = f32[256,1024]{1,0:T(8,128)S(1)} collective-permute-done((f32[256,1024]{1,0:T(8,128)S(1)}, f32[256,1024]{1,0:T(8,128)S(1)}, u32[]{:S(2)}, u32[]{:S(2)}) %collective-permute-start) | collective-permute-done | bytes 1048608 | tf_op jit(solution)/shard_map/ppermute | solution.py:53
  18.7 5.6 %collective-permute-start.7 = (f32[256,1024]{1,0:T(8,128)S(1)}, f32[256,1024]{1,0:T(8,128)S(1)}, u32[]{:S(2)}, u32[]{:S(2)}) collective-permute-start(f32[256,1024]{1,0:T(8,128)S(1)} %collective-permute-done.refs_2_), channel_id=1, source_target_pairs={{0,2},{1,3},{2,4},{3,5},{4,6},{5,7},{6,8},{7,9},{8,10},{9,11},{10,... | collective-permute-start | bytes 3145736 | tf_op jit(solution)/shard_map/ppermute | solution.py:53
  24.4 2.8 %collective-permute-start.2 = (f32[256,256]{1,0:T(8,128)S(1)}, f32[256,256]{1,0:T(8,128)S(1)}, u32[]{:S(2)}, u32[]{:S(2)}) collective-permute-start(f32[256,256]{1,0:T(8,128)S(1)} %constant_dynamic-update-slice_fusion.13), channel_id=1, source_target_pairs={{0,64},{1,65},{2,66},{3,67},{4,68},{5,69},{6,70},{7,71},{8,72},{9,... | collective-permute-start | bytes 786440 | tf_op jit(solution)/shard_map/ppermute | solution.py:53
  28.0 1.7 %collective-permute-done.1 = f32[256,256]{1,0:T(8,128)S(1)} collective-permute-done((f32[256,256]{1,0:T(8,128)S(1)}, f32[256,256]{1,0:T(8,128)S(1)}, u32[]{:S(2)}, u32[]{:S(2)}) %collective-permute-start.1) | collective-permute-done | bytes 262176 | tf_op jit(solution)/shard_map/ppermute | solution.py:53
  29.6 1.6 %collective-permute-done.2 = f32[256,256]{1,0:T(8,128)S(1)} collective-permute-done((f32[256,256]{1,0:T(8,128)S(1)}, f32[256,256]{1,0:T(8,128)S(1)}, u32[]{:S(2)}, u32[]{:S(2)}) %collective-permute-start.2) | collective-permute-done | bytes 262176 | tf_op jit(solution)/shard_map/ppermute | solution.py:53
  31.3 2.8 %collective-permute-done.3 = f32[256,256]{1,0:T(8,128)S(1)} collective-permute-done((f32[256,256]{1,0:T(8,128)S(1)}, f32[256,256]{1,0:T(8,128)S(1)}, u32[]{:S(2)}, u32[]{:S(2)}) %collective-permute-start.3) | collective-permute-done | bytes 262176 | tf_op jit(solution)/shard_map/ppermute | solution.py:53
  35.6 2.2 %collective-permute-start.5 = (f32[4,256,256]{2,1,0:T(8,128)}, f32[4,256,256]{2,1,0:T(8,128)}, u32[]{:S(2)}, u32[]{:S(2)}) collective-permute-start(f32[4,256,256]{2,1,0:T(8,128)} %pad_maximum_fusion), channel_id=1, source_target_pairs={{0,1},{1,128},{2,3},{3,130},{4,5},{5,132},{6,7},{7,134},{8,9},{9,1... | collective-permute-start | bytes 3145736 | tf_op jit(solution)/shard_map/ppermute | solution.py:53
  37.8 2.7 %collective-permute-start.9 = (f32[256,1024]{1,0:T(8,128)S(1)}, f32[256,1024]{1,0:T(8,128)S(1)}, u32[]{:S(2)}, u32[]{:S(2)}) collective-permute-start(f32[256,1024]{1,0:T(8,128)S(1)} %constant_dynamic-update-slice_fusion.11.refs_3_), channel_id=1, source_target_pairs={{0,2},{1,3},{2,4},{3,5},{4,6},{5,7},{6,8},{7,9},{8,10},{9,11},{10,... | collective-permute-start | bytes 3145736 | tf_op jit(solution)/shard_map/ppermute | solution.py:53
  40.6 10.0 %collective-permute-done.4 = f32[4,256,256]{2,1,0:T(8,128)} collective-permute-done((f32[4,256,256]{2,1,0:T(8,128)}, f32[4,256,256]{2,1,0:T(8,128)}, u32[]{:S(2)}, u32[]{:S(2)}) %collective-permute-start.4) | collective-permute-done | bytes 1048608 | tf_op jit(solution)/shard_map/ppermute | solution.py:53
  50.6 1.3 constant_dynamic-update-slice_fusion.12
  53.1 7.1 %collective-permute-done.9 = f32[256,1024]{1,0:T(8,128)S(1)} collective-permute-done((f32[256,1024]{1,0:T(8,128)S(1)}, f32[256,1024]{1,0:T(8,128)S(1)}, u32[]{:S(2)}, u32[]{:S(2)}) %collective-permute-start.9) | collective-permute-done | bytes 1048608 | tf_op jit(solution)/shard_map/ppermute | solution.py:53
  60.9 3.5 %collective-permute-start.12 = (f32[256,1024]{1,0:T(8,128)S(1)}, f32[256,1024]{1,0:T(8,128)S(1)}, u32[]{:S(2)}, u32[]{:S(2)}) collective-permute-start(f32[256,1024]{1,0:T(8,128)S(1)} %constant_dynamic-update-slice_fusion.10.refs_5_), channel_id=1, source_target_pairs={{0,2},{1,3},{2,4},{3,5},{4,6},{5,7},{6,8},{7,9},{8,10},{9,11},{10,... | collective-permute-start | bytes 3145736 | tf_op jit(solution)/shard_map/ppermute | solution.py:53
  64.4 2.6 %collective-permute-done.11.refs_6_ = f32[256,1024]{1,0:T(8,128)} collective-permute-done((f32[256,1024]{1,0:T(8,128)}, f32[256,1024]{1,0:T(8,128)}, u32[]{:S(2)}, u32[]{:S(2)}) %collective-permute-start.11) | collective-permute-done | bytes 1048608 | tf_op jit(solution)/shard_map/ppermute | solution.py:53
  69.9 1.3 constant_dynamic-update-slice_fusion.2
  71.3 1.3 constant_dynamic-update-slice_fusion.refs_1_
  72.6 19.7 %collective-permute-done.13.refs_8_ = f32[256,1024]{1,0:T(8,128)S(1)} collective-permute-done((f32[256,1024]{1,0:T(8,128)}, f32[256,1024]{1,0:T(8,128)S(1)}, u32[]{:S(2)}, u32[]{:S(2)}) %collective-permute-start.13) | collective-permute-done | bytes 1048608 | tf_op jit(solution)/shard_map/ppermute | solution.py:53
  92.6 2.9 %collective-permute-start.14 = (f32[128,1024]{1,0:T(8,128)S(1)}, f32[128,1024]{1,0:T(8,128)S(1)}, u32[]{:S(2)}, u32[]{:S(2)}) collective-permute-start(f32[128,1024]{1,0:T(8,128)S(1)} %slice.94), channel_id=1, source_target_pairs={{0,2},{1,3},{2,4},{3,5},{4,6},{5,7},{6,8},{7,9},{8,10},{9,11},{10,... | collective-permute-start | bytes 1572872 | tf_op jit(solution)/shard_map/ppermute | solution.py:53
  95.5 9.0 %shard_map.68 = f32[512,1024]{1,0:T(8,128)S(1)} custom-call(s32[14]{0:T(128)S(1)} %stack.74.refs_0_, f32[16,256,256]{2,1,0:T(8,128)S(1)} %constant_dynamic-update-slice_fusion.refs_1_, f32[256,1024]{1,0:T(8,128)S(1)} %collective-permute-done.refs_2_, f32[256,1024]{1,0:T(8,128)S(1)} %constant_dynamic-update-slice_fusion.11.refs_3_, ...), custom_call_target="tpu_custom_call" | custom-call | flops 5637144576 | bytes 13631488 | tf_op jit(solution)/shard_map/pallas_call | solution.py:94
  106.8 2.8 %collective-permute-start.16 = (f32[512,1024]{1,0:T(8,128)S(1)}, f32[512,1024]{1,0:T(8,128)}, u32[]{:S(2)}, u32[]{:S(2)}) collective-permute-start(f32[512,1024]{1,0:T(8,128)S(1)} %add.279), channel_id=1, source_target_pairs={{0,16},{1,17},{2,18},{3,19},{4,20},{5,21},{6,22},{7,23},{8,24},{9,... | collective-permute-start | bytes 6291464 | tf_op jit(solution)/shard_map/ppermute | solution.py:53
  109.7 1.8 %maximum_select_fusion = f32[512,1024]{1,0:T(8,128)S(1)} fusion(f32[256,1024]{1,0:T(8,128)} %collective-permute-done.10, f32[256,1024]{1,0:T(8,128)S(1)} %collective-permute-done.refs_2_, pred[]{:T(512)S(6)} %eq.8), kind=kLoop, calls=%fused_computation | loop fusion | flops 1572864 | bytes 4194305 | tf_op jit(solution)/shard_map/jit(_where)/select_n | solution.py:156
  111.5 2.0 %collective-permute-done.16 = f32[512,1024]{1,0:T(8,128)} collective-permute-done((f32[512,1024]{1,0:T(8,128)S(1)}, f32[512,1024]{1,0:T(8,128)}, u32[]{:S(2)}, u32[]{:S(2)}) %collective-permute-start.16) | collective-permute-done | bytes 2097184 | tf_op jit(solution)/shard_map/ppermute | solution.py:53
  113.5 2.0 %add.280 = f32[512,1024]{1,0:T(8,128)S(1)} add(f32[512,1024]{1,0:T(8,128)S(1)} %add.279, f32[512,1024]{1,0:T(8,128)} %collective-permute-done.16) | non-fusion elementwise | flops 524288 | bytes 6291456 | tf_op jit(solution)/shard_map/add | solution.py:174
  117.5 2.7 %collective-permute-start.18 = (f32[64,1024]{1,0:T(8,128)S(1)}, f32[64,1024]{1,0:T(8,128)S(1)}, u32[]{:S(2)}, u32[]{:S(2)}) collective-permute-start(f32[64,1024]{1,0:T(8,128)S(1)} %fusion.11), channel_id=1, source_target_pairs={{0,2},{1,3},{2,4},{3,5},{4,6},{5,7},{6,8},{7,9},{8,10},{9,11},{10,... | collective-permute-start | bytes 786440 | tf_op jit(solution)/shard_map/ppermute | solution.py:53
  120.4 3.7 %collective-permute-done.17 = f32[64,1024]{1,0:T(8,128)S(1)} collective-permute-done((f32[64,1024]{1,0:T(8,128)S(1)}, f32[64,1024]{1,0:T(8,128)S(1)}, u32[]{:S(2)}, u32[]{:S(2)}) %collective-permute-start.17) | collective-permute-done | bytes 262176 | tf_op jit(solution)/shard_map/ppermute | solution.py:53
  126.7 2.2 %collective-permute-start.20 = (f32[64,1024]{1,0:T(8,128)S(1)}, f32[64,1024]{1,0:T(8,128)S(1)}, u32[]{:S(2)}, u32[]{:S(2)}) collective-permute-start(f32[64,1024]{1,0:T(8,128)S(1)} %convolution_add_fusion.4), channel_id=1, source_target_pairs={{0,2},{1,3},{2,4},{3,5},{4,6},{5,7},{6,8},{7,9},{8,10},{9,11},{10,... | collective-permute-start | bytes 786440 | tf_op jit(solution)/shard_map/ppermute | solution.py:53
  128.9 4.3 %collective-permute-start.19 = (f32[256,1024]{1,0:T(8,128)S(1)}, f32[256,1024]{1,0:T(8,128)S(1)}, u32[]{:S(2)}, u32[]{:S(2)}) collective-permute-start(f32[256,1024]{1,0:T(8,128)S(1)} %constant_dynamic-update-slice_fusion.8), channel_id=1, source_target_pairs={{0,0},{1,16},{2,2},{3,18},{4,4},{5,20},{6,6},{7,22},{8,8},{9,24},{... | collective-permute-start | bytes 3145736 | tf_op jit(solution)/shard_map/ppermute | solution.py:53
  135.5 2.7 %collective-permute-start.21 = (f32[64,1024]{1,0:T(8,128)S(1)}, f32[64,1024]{1,0:T(8,128)S(1)}, u32[]{:S(2)}, u32[]{:S(2)}) collective-permute-start(f32[64,1024]{1,0:T(8,128)S(1)} %convolution_add_fusion.2), channel_id=1, source_target_pairs={{0,2},{1,3},{2,4},{3,5},{4,6},{5,7},{6,8},{7,9},{8,10},{9,11},{10,... | collective-permute-start | bytes 786440 | tf_op jit(solution)/shard_map/ppermute | solution.py:53
  138.2 2.7 %collective-permute-done.24 = f32[64,1024]{1,0:T(8,128)S(1)} collective-permute-done((f32[64,1024]{1,0:T(8,128)S(1)}, f32[64,1024]{1,0:T(8,128)S(1)}, u32[]{:S(2)}, u32[]{:S(2)}) %collective-permute-start.24) | collective-permute-done | bytes 262176 | tf_op jit(solution)/shard_map/ppermute | solution.py:53
  141.9 6.7 %collective-permute-start.25 = (f32[64,1024]{1,0:T(8,128)S(1)}, f32[64,1024]{1,0:T(8,128)S(1)}, u32[]{:S(2)}, u32[]{:S(2)}) collective-permute-start(f32[64,1024]{1,0:T(8,128)S(1)} %convolution_add_fusion.1), channel_id=1, source_target_pairs={{0,0},{1,16},{2,2},{3,18},{4,4},{5,20},{6,6},{7,22},{8,8},{9,24},{... | collective-permute-start | bytes 786440 | tf_op jit(solution)/shard_map/ppermute | solution.py:53
  149.6 2.7 %collective-permute-start.22 = (f32[64,1024]{1,0:T(8,128)S(1)}, f32[64,1024]{1,0:T(8,128)S(1)}, u32[]{:S(2)}, u32[]{:S(2)}) collective-permute-start(f32[64,1024]{1,0:T(8,128)S(1)} %constant_dynamic-update-slice_fusion.7), channel_id=1, source_target_pairs={{0,2},{1,18},{2,4},{3,20},{4,6},{5,22},{6,8},{7,24},{8,10},{9,26},... | collective-permute-start | bytes 786440 | tf_op jit(solution)/shard_map/ppermute | solution.py:53
  154.7 2.9 %collective-permute-done.22 = f32[64,1024]{1,0:T(8,128)S(1)} collective-permute-done((f32[64,1024]{1,0:T(8,128)S(1)}, f32[64,1024]{1,0:T(8,128)S(1)}, u32[]{:S(2)}, u32[]{:S(2)}) %collective-permute-start.22) | collective-permute-done | bytes 262176 | tf_op jit(solution)/shard_map/ppermute | solution.py:53
  (78 shorter events, 23.5 us)
Async XLA Ops:
  1.8 16.9 %copy-start = (f32[32,8,4,256]{3,1,2,0:T(8,128)}, f32[32,8,4,256]{3,1,2,0:T(8,128)S(1)}, u32[]{:S(2)}) copy-start(f32[32,8,4,256]{3,1,2,0:T(8,128)S(1)} %copy.7) | copy-start | bytes 3145732
  1.8 22.5 %copy-start.2 = (f32[256,256]{1,0:T(8,128)S(1)}, f32[256,256]{1,0:T(8,128)}, u32[]{:S(2)}) copy-start(f32[256,256]{1,0:T(8,128)} %param.5) | copy-start | bytes 786436
  2.1 16.7 %collective-permute-start = (f32[256,1024]{1,0:T(8,128)S(1)}, f32[256,1024]{1,0:T(8,128)S(1)}, u32[]{:S(2)}, u32[]{:S(2)}) collective-permute-start(f32[256,1024]{1,0:T(8,128)S(1)} %mul.211), channel_id=1, source_target_pairs={{0,0},{1,16},{2,2},{3,18},{4,4},{5,20},{6,6},{7,22},{8,8},{9,24},{... | collective-permute-start | bytes 3145736 | tf_op jit(solution)/shard_map/ppermute | solution.py:53
  18.7 19.1 %collective-permute-start.7 = (f32[256,1024]{1,0:T(8,128)S(1)}, f32[256,1024]{1,0:T(8,128)S(1)}, u32[]{:S(2)}, u32[]{:S(2)}) collective-permute-start(f32[256,1024]{1,0:T(8,128)S(1)} %collective-permute-done.refs_2_), channel_id=1, source_target_pairs={{0,2},{1,3},{2,4},{3,5},{4,6},{5,7},{6,8},{7,9},{8,10},{9,11},{10,... | collective-permute-start | bytes 3145736 | tf_op jit(solution)/shard_map/ppermute | solution.py:53
  24.3 16.2 %collective-permute-start.8 = (f32[256,1024]{1,0:T(8,128)S(1)}, f32[256,1024]{1,0:T(8,128)}, u32[]{:S(2)}, u32[]{:S(2)}) collective-permute-start(f32[256,1024]{1,0:T(8,128)S(1)} %collective-permute-done.refs_2_), channel_id=1, source_target_pairs={{0,14},{1,15},{2,0},{3,1},{4,2},{5,3},{6,4},{7,5},{8,6},{9,7},{10,... | collective-permute-start | bytes 3145736 | tf_op jit(solution)/shard_map/ppermute | solution.py:53
  24.3 5.3 %collective-permute-start.1 = (f32[256,256]{1,0:T(8,128)S(1)}, f32[256,256]{1,0:T(8,128)S(1)}, u32[]{:S(2)}, u32[]{:S(2)}) collective-permute-start(f32[256,256]{1,0:T(8,128)S(1)} %constant_dynamic-update-slice_fusion.13), channel_id=1, source_target_pairs={{0,96},{1,97},{2,98},{3,99},{4,100},{5,101},{6,102},{7,103},{8,104... | collective-permute-start | bytes 786440 | tf_op jit(solution)/shard_map/ppermute | solution.py:53
  24.4 6.9 %collective-permute-start.2 = (f32[256,256]{1,0:T(8,128)S(1)}, f32[256,256]{1,0:T(8,128)S(1)}, u32[]{:S(2)}, u32[]{:S(2)}) collective-permute-start(f32[256,256]{1,0:T(8,128)S(1)} %constant_dynamic-update-slice_fusion.13), channel_id=1, source_target_pairs={{0,64},{1,65},{2,66},{3,67},{4,68},{5,69},{6,70},{7,71},{8,72},{9,... | collective-permute-start | bytes 786440 | tf_op jit(solution)/shard_map/ppermute | solution.py:53
  27.2 6.8 %collective-permute-start.3 = (f32[256,256]{1,0:T(8,128)S(1)}, f32[256,256]{1,0:T(8,128)S(1)}, u32[]{:S(2)}, u32[]{:S(2)}) collective-permute-start(f32[256,256]{1,0:T(8,128)S(1)} %constant_dynamic-update-slice_fusion.13), channel_id=1, source_target_pairs={{0,32},{1,33},{2,34},{3,35},{4,36},{5,37},{6,38},{7,39},{8,40},{9,... | collective-permute-start | bytes 786440 | tf_op jit(solution)/shard_map/ppermute | solution.py:53
  29.6 8.2 %copy-start.3 = (f32[256,256]{1,0:T(8,128)}, f32[256,256]{1,0:T(8,128)S(1)}, u32[]{:S(2)}) copy-start(f32[256,256]{1,0:T(8,128)S(1)} %collective-permute-done.1) | copy-start | bytes 786436
  29.6 23.5 %collective-permute-start.10 = (f32[256,1024]{1,0:T(8,128)S(1)}, f32[256,1024]{1,0:T(8,128)}, u32[]{:S(2)}, u32[]{:S(2)}) collective-permute-start(f32[256,1024]{1,0:T(8,128)S(1)} %collective-permute-done.refs_2_), channel_id=1, source_target_pairs={{0,16},{1,17},{2,18},{3,19},{4,20},{5,21},{6,22},{7,23},{8,24},{9,... | collective-permute-start | bytes 3145736 | tf_op jit(solution)/shard_map/ppermute | solution.py:53
  31.3 6.5 %copy-start.4 = (f32[256,256]{1,0:T(8,128)}, f32[256,256]{1,0:T(8,128)S(1)}, u32[]{:S(2)}) copy-start(f32[256,256]{1,0:T(8,128)S(1)} %collective-permute-done.2) | copy-start | bytes 786436
  35.1 15.5 %collective-permute-start.4 = (f32[4,256,256]{2,1,0:T(8,128)}, f32[4,256,256]{2,1,0:T(8,128)}, u32[]{:S(2)}, u32[]{:S(2)}) collective-permute-start(f32[4,256,256]{2,1,0:T(8,128)} %pad_maximum_fusion), channel_id=1, source_target_pairs={{0,129},{1,0},{2,131},{3,2},{4,133},{5,4},{6,135},{7,6},{8,137},{9... | collective-permute-start | bytes 3145736 | tf_op jit(solution)/shard_map/ppermute | solution.py:53
  35.6 15.0 %collective-permute-start.5 = (f32[4,256,256]{2,1,0:T(8,128)}, f32[4,256,256]{2,1,0:T(8,128)}, u32[]{:S(2)}, u32[]{:S(2)}) collective-permute-start(f32[4,256,256]{2,1,0:T(8,128)} %pad_maximum_fusion), channel_id=1, source_target_pairs={{0,1},{1,128},{2,3},{3,130},{4,5},{5,132},{6,7},{7,134},{8,9},{9,1... | collective-permute-start | bytes 3145736 | tf_op jit(solution)/shard_map/ppermute | solution.py:53
  37.8 22.3 %collective-permute-start.9 = (f32[256,1024]{1,0:T(8,128)S(1)}, f32[256,1024]{1,0:T(8,128)S(1)}, u32[]{:S(2)}, u32[]{:S(2)}) collective-permute-start(f32[256,1024]{1,0:T(8,128)S(1)} %constant_dynamic-update-slice_fusion.11.refs_3_), channel_id=1, source_target_pairs={{0,2},{1,3},{2,4},{3,5},{4,6},{5,7},{6,8},{7,9},{8,10},{9,11},{10,... | collective-permute-start | bytes 3145736 | tf_op jit(solution)/shard_map/ppermute | solution.py:53
  40.5 26.4 %collective-permute-start.11 = (f32[256,1024]{1,0:T(8,128)}, f32[256,1024]{1,0:T(8,128)}, u32[]{:S(2)}, u32[]{:S(2)}) collective-permute-start(f32[256,1024]{1,0:T(8,128)} %collective-permute-done.8.refs_4_), channel_id=1, source_target_pairs={{0,14},{1,15},{2,0},{3,1},{4,2},{5,3},{6,4},{7,5},{8,6},{9,7},{10,... | collective-permute-start | bytes 3145736 | tf_op jit(solution)/shard_map/ppermute | solution.py:53
  51.9 19.3 %collective-permute-start.6 = (f32[4,256,256]{2,1,0:T(8,128)}, f32[4,256,256]{2,1,0:T(8,128)S(1)}, u32[]{:S(2)}, u32[]{:S(2)}) collective-permute-start(f32[4,256,256]{2,1,0:T(8,128)} %constant_dynamic-update-slice_fusion.12), channel_id=1, source_target_pairs={{0,128},{1,129},{2,130},{3,131},{4,132},{5,133},{6,134},{7,135},{8... | collective-permute-start | bytes 3145736 | tf_op jit(solution)/shard_map/ppermute | solution.py:53
  60.9 31.6 %collective-permute-start.12 = (f32[256,1024]{1,0:T(8,128)S(1)}, f32[256,1024]{1,0:T(8,128)S(1)}, u32[]{:S(2)}, u32[]{:S(2)}) collective-permute-start(f32[256,1024]{1,0:T(8,128)S(1)} %constant_dynamic-update-slice_fusion.10.refs_5_), channel_id=1, source_target_pairs={{0,2},{1,3},{2,4},{3,5},{4,6},{5,7},{6,8},{7,9},{8,10},{9,11},{10,... | collective-permute-start | bytes 3145736 | tf_op jit(solution)/shard_map/ppermute | solution.py:53
  67.0 25.4 %collective-permute-start.13 = (f32[256,1024]{1,0:T(8,128)}, f32[256,1024]{1,0:T(8,128)S(1)}, u32[]{:S(2)}, u32[]{:S(2)}) collective-permute-start(f32[256,1024]{1,0:T(8,128)} %collective-permute-done.11.refs_6_), channel_id=1, source_target_pairs={{0,14},{1,15},{2,0},{3,1},{4,2},{5,3},{6,4},{7,5},{8,6},{9,7},{10,... | collective-permute-start | bytes 3145736 | tf_op jit(solution)/shard_map/ppermute | solution.py:53
  92.4 12.9 %collective-permute-start.15 = (f32[128,1024]{1,0:T(8,128)S(1)}, f32[128,1024]{1,0:T(8,128)S(1)}, u32[]{:S(2)}, u32[]{:S(2)}) collective-permute-start(f32[128,1024]{1,0:T(8,128)S(1)} %slice.95), channel_id=1, source_target_pairs={{0,14},{1,15},{2,0},{3,1},{4,2},{5,3},{6,4},{7,5},{8,6},{9,7},{10,... | collective-permute-start | bytes 1572872 | tf_op jit(solution)/shard_map/ppermute | solution.py:53
  92.6 12.8 %collective-permute-start.14 = (f32[128,1024]{1,0:T(8,128)S(1)}, f32[128,1024]{1,0:T(8,128)S(1)}, u32[]{:S(2)}, u32[]{:S(2)}) collective-permute-start(f32[128,1024]{1,0:T(8,128)S(1)} %slice.94), channel_id=1, source_target_pairs={{0,2},{1,3},{2,4},{3,5},{4,6},{5,7},{6,8},{7,9},{8,10},{9,11},{10,... | collective-permute-start | bytes 1572872 | tf_op jit(solution)/shard_map/ppermute | solution.py:53
  106.8 6.7 %collective-permute-start.16 = (f32[512,1024]{1,0:T(8,128)S(1)}, f32[512,1024]{1,0:T(8,128)}, u32[]{:S(2)}, u32[]{:S(2)}) collective-permute-start(f32[512,1024]{1,0:T(8,128)S(1)} %add.279), channel_id=1, source_target_pairs={{0,16},{1,17},{2,18},{3,19},{4,20},{5,21},{6,22},{7,23},{8,24},{9,... | collective-permute-start | bytes 6291464 | tf_op jit(solution)/shard_map/ppermute | solution.py:53
  116.5 7.6 %collective-permute-start.17 = (f32[64,1024]{1,0:T(8,128)S(1)}, f32[64,1024]{1,0:T(8,128)S(1)}, u32[]{:S(2)}, u32[]{:S(2)}) collective-permute-start(f32[64,1024]{1,0:T(8,128)S(1)} %fusion.14), channel_id=1, source_target_pairs={{0,14},{1,15},{2,0},{3,1},{4,2},{5,3},{6,4},{7,5},{8,6},{9,7},{10,... | collective-permute-start | bytes 786440 | tf_op jit(solution)/shard_map/ppermute | solution.py:53
  117.5 8.2 %collective-permute-start.18 = (f32[64,1024]{1,0:T(8,128)S(1)}, f32[64,1024]{1,0:T(8,128)S(1)}, u32[]{:S(2)}, u32[]{:S(2)}) collective-permute-start(f32[64,1024]{1,0:T(8,128)S(1)} %fusion.11), channel_id=1, source_target_pairs={{0,2},{1,3},{2,4},{3,5},{4,6},{5,7},{6,8},{7,9},{8,10},{9,11},{10,... | collective-permute-start | bytes 786440 | tf_op jit(solution)/shard_map/ppermute | solution.py:53
  125.1 8.1 %collective-permute-start.23 = (f32[64,1024]{1,0:T(8,128)S(1)}, f32[64,1024]{1,0:T(8,128)S(1)}, u32[]{:S(2)}, u32[]{:S(2)}) collective-permute-start(f32[64,1024]{1,0:T(8,128)S(1)} %convolution_add_fusion.5), channel_id=1, source_target_pairs={{0,14},{1,15},{2,0},{3,1},{4,2},{5,3},{6,4},{7,5},{8,6},{9,7},{10,... | collective-permute-start | bytes 786440 | tf_op jit(solution)/shard_map/ppermute | solution.py:53
  126.7 7.8 %collective-permute-start.20 = (f32[64,1024]{1,0:T(8,128)S(1)}, f32[64,1024]{1,0:T(8,128)S(1)}, u32[]{:S(2)}, u32[]{:S(2)}) collective-permute-start(f32[64,1024]{1,0:T(8,128)S(1)} %convolution_add_fusion.4), channel_id=1, source_target_pairs={{0,2},{1,3},{2,4},{3,5},{4,6},{5,7},{6,8},{7,9},{8,10},{9,11},{10,... | collective-permute-start | bytes 786440 | tf_op jit(solution)/shard_map/ppermute | solution.py:53
  128.9 20.7 %collective-permute-start.19 = (f32[256,1024]{1,0:T(8,128)S(1)}, f32[256,1024]{1,0:T(8,128)S(1)}, u32[]{:S(2)}, u32[]{:S(2)}) collective-permute-start(f32[256,1024]{1,0:T(8,128)S(1)} %constant_dynamic-update-slice_fusion.8), channel_id=1, source_target_pairs={{0,0},{1,16},{2,2},{3,18},{4,4},{5,20},{6,6},{7,22},{8,8},{9,24},{... | collective-permute-start | bytes 3145736 | tf_op jit(solution)/shard_map/ppermute | solution.py:53
  134.2 6.7 %collective-permute-start.24 = (f32[64,1024]{1,0:T(8,128)S(1)}, f32[64,1024]{1,0:T(8,128)S(1)}, u32[]{:S(2)}, u32[]{:S(2)}) collective-permute-start(f32[64,1024]{1,0:T(8,128)S(1)} %convolution_add_fusion), channel_id=1, source_target_pairs={{0,14},{1,15},{2,0},{3,1},{4,2},{5,3},{6,4},{7,5},{8,6},{9,7},{10,... | collective-permute-start | bytes 786440 | tf_op jit(solution)/shard_map/ppermute | solution.py:53
  135.5 13.1 %collective-permute-start.21 = (f32[64,1024]{1,0:T(8,128)S(1)}, f32[64,1024]{1,0:T(8,128)S(1)}, u32[]{:S(2)}, u32[]{:S(2)}) collective-permute-start(f32[64,1024]{1,0:T(8,128)S(1)} %convolution_add_fusion.2), channel_id=1, source_target_pairs={{0,2},{1,3},{2,4},{3,5},{4,6},{5,7},{6,8},{7,9},{8,10},{9,11},{10,... | collective-permute-start | bytes 786440 | tf_op jit(solution)/shard_map/ppermute | solution.py:53
  141.9 10.5 %copy-start.1 = (f32[32,8,4,256]{3,1,2,0:T(8,128)S(1)}, f32[32,8,4,256]{3,1,2,0:T(8,128)}, u32[]{:S(2)}) copy-start(f32[32,8,4,256]{3,1,2,0:T(8,128)} %copy-done) | copy-start | bytes 3145732
  141.9 12.8 %collective-permute-start.25 = (f32[64,1024]{1,0:T(8,128)S(1)}, f32[64,1024]{1,0:T(8,128)S(1)}, u32[]{:S(2)}, u32[]{:S(2)}) collective-permute-start(f32[64,1024]{1,0:T(8,128)S(1)} %convolution_add_fusion.1), channel_id=1, source_target_pairs={{0,0},{1,16},{2,2},{3,18},{4,4},{5,20},{6,6},{7,22},{8,8},{9,24},{... | collective-permute-start | bytes 786440 | tf_op jit(solution)/shard_map/ppermute | solution.py:53
  149.6 8.0 %copy-start.7 = (f32[64,1024]{1,0:T(8,128)S(1)}, f32[64,1024]{1,0:T(8,128)}, u32[]{:S(2)}) copy-start(f32[64,1024]{1,0:T(8,128)} %param.9) | copy-start | bytes 786436
  149.6 8.0 %collective-permute-start.22 = (f32[64,1024]{1,0:T(8,128)S(1)}, f32[64,1024]{1,0:T(8,128)S(1)}, u32[]{:S(2)}, u32[]{:S(2)}) collective-permute-start(f32[64,1024]{1,0:T(8,128)S(1)} %constant_dynamic-update-slice_fusion.7), channel_id=1, source_target_pairs={{0,2},{1,18},{2,4},{3,20},{4,6},{5,22},{6,8},{7,24},{8,10},{9,26},... | collective-permute-start | bytes 786440 | tf_op jit(solution)/shard_map/ppermute | solution.py:53
  (3 other events, 8.2 us)

commit v3 on v2

--- a/solution.py
+++ b/solution.py
@@ -173,9 +173,19 @@
     total = total + dot(opposite, jnp.concatenate([last, last_astern]))
     total = total + send(total, swap_cores())
 
+    total_high = lax.reduce_precision(total, 8, 7)
+    total_low = (total - total_high).astype(jnp.bfloat16)
+    total_high = total_high.astype(jnp.bfloat16)
+    right = jnp.concatenate([total_high, total_low, total_high])
+
     def term(zk):
         at = (zk & 7) * 128 + core * 64
-        return dot(lax.dynamic_slice(columns, (at, 0), (64, 2 * ROWS)), total)
+        left = lax.dynamic_slice(columns, (at, 0), (64, 2 * ROWS))
+        high = lax.reduce_precision(left, 8, 7)
+        low = (left - high).astype(jnp.bfloat16)
+        high = high.astype(jnp.bfloat16)
+        joined = jnp.concatenate([high, high, low], axis=1)
+        return jnp.dot(joined, right, preferred_element_type=jnp.float32)
 
     def step_of(far_sum, near_sum, step):
         arrived = [send(far_sum, ring(1)), send(near_sum, ring(-1))]
@@ -183,10 +193,10 @@
 
     far_sum, near_sum = step_of(term(z + way * 4), term(z - way * 3), 3)
     piece = lax.dynamic_slice(total, (core * ROWS, 0), (ROWS, 4 * ROWS))
-    out = send(after(piece, [far_sum, near_sum]), to_home(0))
+    out = send(lax.optimization_barrier((piece, far_sum, near_sum))[0], to_home(0))
     far_sum, near_sum = step_of(far_sum, near_sum, 2)
     far_sum, near_sum = step_of(far_sum, near_sum, 1)
-    far_sum = after(far_sum, [out])
+    far_sum, out = lax.optimization_barrier((far_sum, out))
     sums = send(far_sum, to_home(1)) + send(near_sum, to_home(0))
 
     offdiag = -out * mask

time: 159 us -> 157 us (0.987)
  matrix products: 8.86 us -> 6.57 us
    dot_general x9 -> x1, matrix products: 8.86 us -> 1.04 us  [dot(): return jnp.dot(a, b, precision=HIGH, preferred_element_type=jnp.float32)]
    dot_general x0 -> x8, matrix products: none -> 5.53 us  [term(): return jnp.dot(joined, right, preferred_element_type=jnp.float32)]
    convert_element_type x0 -> x3, other arithmetic: none -> 2.97 us  [the longest x1 2.13 us: shards(): total_low = (total - total_high).astype(jnp.bfloat16)]
    add x1 -> x0, other arithmetic: 1.98 us -> none  [shards(): total = total + send(total, swap_cores())]
  transfers between devices with their start and end apart: 26 -> 26, of which waited for: 15 -> 15; matrix products, arithmetic and copies ran while one was open for 12% -> 11% of each run, Pallas kernels for 6% -> 6%
where the time goes in v3:
time: 157 us
  waiting for transfers between devices  71.8 us (46%)
  starting transfers between devices  50.9 us (32%)
  other arithmetic  11.1 us (7%)
  Pallas kernels  8.99 us (6%)
  matrix products  6.57 us (4%)
  local copies, waits for them, and re-layouts  6.46 us (4%)
    ppermute x26, waiting for transfers between devices, send(): return lax.ppermute(value, AXES, perm)  71.8 us
    ppermute x26, starting transfers between devices, send(): return lax.ppermute(value, AXES, perm)  50.9 us
    pallas_call x1, Pallas kernels, products(): pl.pallas_call(lambda *refs: product_kernel(count, *refs), grid_spec=pltp...  8.99 us
    dot_general x8, matrix products, term(): return jnp.dot(joined, right, preferred_element_type=jnp.float32)  5.53 us
    unnamed x25, local copies, waits for them, and re-layouts  4.57 us
  transfers between devices with their start and end apart: 26, of which 15 were waited for; matrix products, arithmetic and copies ran while one was open for 11% of the time, Pallas kernels for 6%

profile of v3, /device:TPU:25, one launch (start us, length us, event | category | flops | bytes accessed | tf_op | source)
XLA Modules:
  0.0 156.9 jit_solution(2869702927436226147)
XLA Ops:
  2.1 3.7 %collective-permute-start = (f32[256,1024]{1,0:T(8,128)S(1)}, f32[256,1024]{1,0:T(8,128)S(1)}, u32[]{:S(2)}, u32[]{:S(2)}) collective-permute-start(f32[256,1024]{1,0:T(8,128)S(1)} %mul.179), channel_id=1, source_target_pairs={{0,0},{1,16},{2,2},{3,18},{4,4},{5,20},{6,6},{7,22},{8,8},{9,24},{... | collective-permute-start | bytes 3145736 | tf_op jit(solution)/shard_map/ppermute | solution.py:53
  5.7 12.9 %collective-permute-done.refs_2_ = f32[256,1024]{1,0:T(8,128)S(1)} collective-permute-done((f32[256,1024]{1,0:T(8,128)S(1)}, f32[256,1024]{1,0:T(8,128)S(1)}, u32[]{:S(2)}, u32[]{:S(2)}) %collective-permute-start) | collective-permute-done | bytes 1048608 | tf_op jit(solution)/shard_map/ppermute | solution.py:53
  18.6 5.6 %collective-permute-start.8 = (f32[256,1024]{1,0:T(8,128)S(1)}, f32[256,1024]{1,0:T(8,128)S(1)}, u32[]{:S(2)}, u32[]{:S(2)}) collective-permute-start(f32[256,1024]{1,0:T(8,128)S(1)} %collective-permute-done.refs_2_), channel_id=1, source_target_pairs={{0,2},{1,3},{2,4},{3,5},{4,6},{5,7},{6,8},{7,9},{8,10},{9,11},{10,... | collective-permute-start | bytes 3145736 | tf_op jit(solution)/shard_map/ppermute | solution.py:53
  24.3 2.8 %collective-permute-start.3 = (f32[256,256]{1,0:T(8,128)S(1)}, f32[256,256]{1,0:T(8,128)S(1)}, u32[]{:S(2)}, u32[]{:S(2)}) collective-permute-start(f32[256,256]{1,0:T(8,128)S(1)} %fusion.83), channel_id=1, source_target_pairs={{0,64},{1,65},{2,66},{3,67},{4,68},{5,69},{6,70},{7,71},{8,72},{9,... | collective-permute-start | bytes 786440 | tf_op jit(solution)/shard_map/ppermute | solution.py:53
  27.8 1.7 %collective-permute-done.2 = f32[256,256]{1,0:T(8,128)S(1)} collective-permute-done((f32[256,256]{1,0:T(8,128)S(1)}, f32[256,256]{1,0:T(8,128)S(1)}, u32[]{:S(2)}, u32[]{:S(2)}) %collective-permute-start.2) | collective-permute-done | bytes 262176 | tf_op jit(solution)/shard_map/ppermute | solution.py:53
  29.5 1.6 %collective-permute-done.3 = f32[256,256]{1,0:T(8,128)S(1)} collective-permute-done((f32[256,256]{1,0:T(8,128)S(1)}, f32[256,256]{1,0:T(8,128)S(1)}, u32[]{:S(2)}, u32[]{:S(2)}) %collective-permute-start.3) | collective-permute-done | bytes 262176 | tf_op jit(solution)/shard_map/ppermute | solution.py:53
  31.1 2.8 %collective-permute-done.4 = f32[256,256]{1,0:T(8,128)S(1)} collective-permute-done((f32[256,256]{1,0:T(8,128)S(1)}, f32[256,256]{1,0:T(8,128)S(1)}, u32[]{:S(2)}, u32[]{:S(2)}) %collective-permute-start.4) | collective-permute-done | bytes 262176 | tf_op jit(solution)/shard_map/ppermute | solution.py:53
  35.5 2.2 %collective-permute-start.6 = (f32[4,256,256]{2,1,0:T(8,128)}, f32[4,256,256]{2,1,0:T(8,128)}, u32[]{:S(2)}, u32[]{:S(2)}) collective-permute-start(f32[4,256,256]{2,1,0:T(8,128)} %pad_maximum_fusion.1), channel_id=1, source_target_pairs={{0,1},{1,128},{2,3},{3,130},{4,5},{5,132},{6,7},{7,134},{8,9},{9,1... | collective-permute-start | bytes 3145736 | tf_op jit(solution)/shard_map/ppermute | solution.py:53
  37.7 2.7 %collective-permute-start.10 = (f32[256,1024]{1,0:T(8,128)S(1)}, f32[256,1024]{1,0:T(8,128)S(1)}, u32[]{:S(2)}, u32[]{:S(2)}) collective-permute-start(f32[256,1024]{1,0:T(8,128)S(1)} %fusion.80.refs_3_), channel_id=1, source_target_pairs={{0,2},{1,3},{2,4},{3,5},{4,6},{5,7},{6,8},{7,9},{8,10},{9,11},{10,... | collective-permute-start | bytes 3145736 | tf_op jit(solution)/shard_map/ppermute | solution.py:53
  40.5 10.0 %collective-permute-done.5 = f32[4,256,256]{2,1,0:T(8,128)} collective-permute-done((f32[4,256,256]{2,1,0:T(8,128)}, f32[4,256,256]{2,1,0:T(8,128)}, u32[]{:S(2)}, u32[]{:S(2)}) %collective-permute-start.5) | collective-permute-done | bytes 1048608 | tf_op jit(solution)/shard_map/ppermute | solution.py:53
  50.5 1.3 fusion.82
  53.0 7.1 %collective-permute-done.10 = f32[256,1024]{1,0:T(8,128)S(1)} collective-permute-done((f32[256,1024]{1,0:T(8,128)S(1)}, f32[256,1024]{1,0:T(8,128)S(1)}, u32[]{:S(2)}, u32[]{:S(2)}) %collective-permute-start.10) | collective-permute-done | bytes 1048608 | tf_op jit(solution)/shard_map/ppermute | solution.py:53
  60.8 3.5 %collective-permute-start.12 = (f32[256,1024]{1,0:T(8,128)S(1)}, f32[256,1024]{1,0:T(8,128)S(1)}, u32[]{:S(2)}, u32[]{:S(2)}) collective-permute-start(f32[256,1024]{1,0:T(8,128)S(1)} %fusion.77.refs_5_), channel_id=1, source_target_pairs={{0,2},{1,3},{2,4},{3,5},{4,6},{5,7},{6,8},{7,9},{8,10},{9,11},{10,... | collective-permute-start | bytes 3145736 | tf_op jit(solution)/shard_map/ppermute | solution.py:53
  64.3 2.6 %collective-permute-done.11.refs_6_ = f32[256,1024]{1,0:T(8,128)} collective-permute-done((f32[256,1024]{1,0:T(8,128)}, f32[256,1024]{1,0:T(8,128)}, u32[]{:S(2)}, u32[]{:S(2)}) %collective-permute-start.11) | collective-permute-done | bytes 1048608 | tf_op jit(solution)/shard_map/ppermute | solution.py:53
  69.7 1.3 constant_dynamic-update-slice_fusion.2
  71.1 1.3 constant_dynamic-update-slice_fusion.refs_1_
  72.5 19.7 %collective-permute-done.13.refs_8_ = f32[256,1024]{1,0:T(8,128)S(1)} collective-permute-done((f32[256,1024]{1,0:T(8,128)}, f32[256,1024]{1,0:T(8,128)S(1)}, u32[]{:S(2)}, u32[]{:S(2)}) %collective-permute-start.13) | collective-permute-done | bytes 1048608 | tf_op jit(solution)/shard_map/ppermute | solution.py:53
  92.4 2.9 %collective-permute-start.14 = (f32[128,1024]{1,0:T(8,128)S(1)}, f32[128,1024]{1,0:T(8,128)S(1)}, u32[]{:S(2)}, u32[]{:S(2)}) collective-permute-start(f32[128,1024]{1,0:T(8,128)S(1)} %slice.74), channel_id=1, source_target_pairs={{0,2},{1,3},{2,4},{3,5},{4,6},{5,7},{6,8},{7,9},{8,10},{9,11},{10,... | collective-permute-start | bytes 1572872 | tf_op jit(solution)/shard_map/ppermute | solution.py:53
  95.3 9.0 %shard_map.68 = f32[512,1024]{1,0:T(8,128)S(1)} custom-call(s32[14]{0:T(128)S(1)} %stack.74.refs_0_, f32[16,256,256]{2,1,0:T(8,128)S(1)} %constant_dynamic-update-slice_fusion.refs_1_, f32[256,1024]{1,0:T(8,128)S(1)} %collective-permute-done.refs_2_, f32[256,1024]{1,0:T(8,128)S(1)} %fusion.80.refs_3_, f32[256,1024]{1,0:T(8,128)} %collective-permute-done.9.refs_4_, ...), custom_call_target="tpu_custom_call" | custom-call | flops 5637144576 | bytes 13631488 | tf_op jit(solution)/shard_map/pallas_call | solution.py:94
  106.6 2.8 %collective-permute-start.16 = (f32[512,1024]{1,0:T(8,128)S(1)}, f32[512,1024]{1,0:T(8,128)}, u32[]{:S(2)}, u32[]{:S(2)}) collective-permute-start(f32[512,1024]{1,0:T(8,128)S(1)} %add.281), channel_id=1, source_target_pairs={{0,16},{1,17},{2,18},{3,19},{4,20},{5,21},{6,22},{7,23},{8,24},{9,... | collective-permute-start | bytes 6291464 | tf_op jit(solution)/shard_map/ppermute | solution.py:53
  109.5 1.8 %maximum_select_fusion = f32[512,1024]{1,0:T(8,128)S(1)} fusion(f32[256,1024]{1,0:T(8,128)} %collective-permute-done.1, f32[256,1024]{1,0:T(8,128)S(1)} %collective-permute-done.refs_2_, pred[]{:T(512)S(6)} %eq.8), kind=kLoop, calls=%fused_computation.4 | loop fusion | flops 1572864 | bytes 4194305 | tf_op jit(solution)/shard_map/jit(_where)/select_n | solution.py:156
  112.0 1.3 collective-permute-done.16
  113.4 2.1 %fusion = (bf16[512,1024]{1,0:T(8,128)(2,1)S(1)}, f32[512,1024]{1,0:T(8,128)S(1)}) fusion(f32[512,1024]{1,0:T(8,128)S(1)} %add.281, f32[512,1024]{1,0:T(8,128)} %collective-permute-done.16), kind=kLoop, calls=%fused_computation.3 | loop fusion | flops 2097152 | bytes 7340032 | tf_op jit(solution)/shard_map/convert_element_type | solution.py:177
  117.1 2.7 %collective-permute-start.17 = (f32[64,1024]{1,0:T(8,128)S(1)}, f32[64,1024]{1,0:T(8,128)S(1)}, u32[]{:S(2)}, u32[]{:S(2)}) collective-permute-start(f32[64,1024]{1,0:T(8,128)S(1)} %fusion.31), channel_id=1, source_target_pairs={{0,2},{1,3},{2,4},{3,5},{4,6},{5,7},{6,8},{7,9},{8,10},{9,11},{10,... | collective-permute-start | bytes 786440 | tf_op jit(solution)/shard_map/ppermute | solution.py:53
  120.0 4.3 %collective-permute-done.20 = f32[64,1024]{1,0:T(8,128)S(1)} collective-permute-done((f32[64,1024]{1,0:T(8,128)S(1)}, f32[64,1024]{1,0:T(8,128)S(1)}, u32[]{:S(2)}, u32[]{:S(2)}) %collective-permute-start.20) | collective-permute-done | bytes 262176 | tf_op jit(solution)/shard_map/ppermute | solution.py:53
  126.2 2.3 %collective-permute-start.18 = (f32[64,1024]{1,0:T(8,128)S(1)}, f32[64,1024]{1,0:T(8,128)S(1)}, u32[]{:S(2)}, u32[]{:S(2)}) collective-permute-start(f32[64,1024]{1,0:T(8,128)S(1)} %convolution_add_fusion.1), channel_id=1, source_target_pairs={{0,2},{1,3},{2,4},{3,5},{4,6},{5,7},{6,8},{7,9},{8,10},{9,11},{10,... | collective-permute-start | bytes 786440 | tf_op jit(solution)/shard_map/ppermute | solution.py:53
  128.5 4.2 %collective-permute-start.21 = (f32[256,1024]{1,0:T(8,128)S(1)}, f32[256,1024]{1,0:T(8,128)S(1)}, u32[]{:S(2)}, u32[]{:S(2)}) collective-permute-start(f32[256,1024]{1,0:T(8,128)S(1)} %constant_dynamic-slice_fusion), channel_id=1, source_target_pairs={{0,0},{1,16},{2,2},{3,18},{4,4},{5,20},{6,6},{7,22},{8,8},{9,24},{... | collective-permute-start | bytes 3145736 | tf_op jit(solution)/shard_map/ppermute | solution.py:53
  134.5 2.7 %collective-permute-start.19 = (f32[64,1024]{1,0:T(8,128)S(1)}, f32[64,1024]{1,0:T(8,128)S(1)}, u32[]{:S(2)}, u32[]{:S(2)}) collective-permute-start(f32[64,1024]{1,0:T(8,128)S(1)} %fusion.19), channel_id=1, source_target_pairs={{0,2},{1,3},{2,4},{3,5},{4,6},{5,7},{6,8},{7,9},{8,10},{9,11},{10,... | collective-permute-start | bytes 786440 | tf_op jit(solution)/shard_map/ppermute | solution.py:53
  137.2 3.0 %collective-permute-done.24 = f32[64,1024]{1,0:T(8,128)S(1)} collective-permute-done((f32[64,1024]{1,0:T(8,128)S(1)}, f32[64,1024]{1,0:T(8,128)S(1)}, u32[]{:S(2)}, u32[]{:S(2)}) %collective-permute-start.24) | collective-permute-done | bytes 262176 | tf_op jit(solution)/shard_map/ppermute | solution.py:53
  140.9 6.5 %collective-permute-start.25 = (f32[64,1024]{1,0:T(8,128)S(1)}, f32[64,1024]{1,0:T(8,128)S(1)}, u32[]{:S(2)}, u32[]{:S(2)}) collective-permute-start(f32[64,1024]{1,0:T(8,128)S(1)} %fusion.50), channel_id=1, source_target_pairs={{0,0},{1,16},{2,2},{3,18},{4,4},{5,20},{6,6},{7,22},{8,8},{9,24},{... | collective-permute-start | bytes 786440 | tf_op jit(solution)/shard_map/ppermute | solution.py:53
  148.1 3.2 %collective-permute-start.22 = (f32[64,1024]{1,0:T(8,128)S(1)}, f32[64,1024]{1,0:T(8,128)S(1)}, u32[]{:S(2)}, u32[]{:S(2)}) collective-permute-start(f32[64,1024]{1,0:T(8,128)S(1)} %fusion.10), channel_id=1, source_target_pairs={{0,2},{1,18},{2,4},{3,20},{4,6},{5,22},{6,8},{7,24},{8,10},{9,26},... | collective-permute-start | bytes 786440 | tf_op jit(solution)/shard_map/ppermute | solution.py:53
  153.5 2.6 %collective-permute-done.22 = f32[64,1024]{1,0:T(8,128)S(1)} collective-permute-done((f32[64,1024]{1,0:T(8,128)S(1)}, f32[64,1024]{1,0:T(8,128)S(1)}, u32[]{:S(2)}, u32[]{:S(2)}) %collective-permute-start.22) | collective-permute-done | bytes 262176 | tf_op jit(solution)/shard_map/ppermute | solution.py:53
  (78 shorter events, 21.7 us)
Async XLA Ops:
  1.4 22.8 %copy-start.2 = (f32[256,256]{1,0:T(8,128)S(1)}, f32[256,256]{1,0:T(8,128)}, u32[]{:S(2)}) copy-start(f32[256,256]{1,0:T(8,128)} %param.5) | copy-start | bytes 786436
  1.8 16.8 %copy-start = (f32[32,8,4,256]{3,1,2,0:T(8,128)}, f32[32,8,4,256]{3,1,2,0:T(8,128)S(1)}, u32[]{:S(2)}) copy-start(f32[32,8,4,256]{3,1,2,0:T(8,128)S(1)} %copy.7) | copy-start | bytes 3145732
  2.1 16.6 %collective-permute-start = (f32[256,1024]{1,0:T(8,128)S(1)}, f32[256,1024]{1,0:T(8,128)S(1)}, u32[]{:S(2)}, u32[]{:S(2)}) collective-permute-start(f32[256,1024]{1,0:T(8,128)S(1)} %mul.179), channel_id=1, source_target_pairs={{0,0},{1,16},{2,2},{3,18},{4,4},{5,20},{6,6},{7,22},{8,8},{9,24},{... | collective-permute-start | bytes 3145736 | tf_op jit(solution)/shard_map/ppermute | solution.py:53
  18.6 19.1 %collective-permute-start.8 = (f32[256,1024]{1,0:T(8,128)S(1)}, f32[256,1024]{1,0:T(8,128)S(1)}, u32[]{:S(2)}, u32[]{:S(2)}) collective-permute-start(f32[256,1024]{1,0:T(8,128)S(1)} %collective-permute-done.refs_2_), channel_id=1, source_target_pairs={{0,2},{1,3},{2,4},{3,5},{4,6},{5,7},{6,8},{7,9},{8,10},{9,11},{10,... | collective-permute-start | bytes 3145736 | tf_op jit(solution)/shard_map/ppermute | solution.py:53
  24.2 16.2 %collective-permute-start.9 = (f32[256,1024]{1,0:T(8,128)S(1)}, f32[256,1024]{1,0:T(8,128)}, u32[]{:S(2)}, u32[]{:S(2)}) collective-permute-start(f32[256,1024]{1,0:T(8,128)S(1)} %collective-permute-done.refs_2_), channel_id=1, source_target_pairs={{0,14},{1,15},{2,0},{3,1},{4,2},{5,3},{6,4},{7,5},{8,6},{9,7},{10,... | collective-permute-start | bytes 3145736 | tf_op jit(solution)/shard_map/ppermute | solution.py:53
  24.2 5.3 %collective-permute-start.2 = (f32[256,256]{1,0:T(8,128)S(1)}, f32[256,256]{1,0:T(8,128)S(1)}, u32[]{:S(2)}, u32[]{:S(2)}) collective-permute-start(f32[256,256]{1,0:T(8,128)S(1)} %fusion.83), channel_id=1, source_target_pairs={{0,96},{1,97},{2,98},{3,99},{4,100},{5,101},{6,102},{7,103},{8,104... | collective-permute-start | bytes 786440 | tf_op jit(solution)/shard_map/ppermute | solution.py:53
  24.3 6.9 %collective-permute-start.3 = (f32[256,256]{1,0:T(8,128)S(1)}, f32[256,256]{1,0:T(8,128)S(1)}, u32[]{:S(2)}, u32[]{:S(2)}) collective-permute-start(f32[256,256]{1,0:T(8,128)S(1)} %fusion.83), channel_id=1, source_target_pairs={{0,64},{1,65},{2,66},{3,67},{4,68},{5,69},{6,70},{7,71},{8,72},{9,... | collective-permute-start | bytes 786440 | tf_op jit(solution)/shard_map/ppermute | solution.py:53
  27.1 6.8 %collective-permute-start.4 = (f32[256,256]{1,0:T(8,128)S(1)}, f32[256,256]{1,0:T(8,128)S(1)}, u32[]{:S(2)}, u32[]{:S(2)}) collective-permute-start(f32[256,256]{1,0:T(8,128)S(1)} %fusion.83), channel_id=1, source_target_pairs={{0,32},{1,33},{2,34},{3,35},{4,36},{5,37},{6,38},{7,39},{8,40},{9,... | collective-permute-start | bytes 786440 | tf_op jit(solution)/shard_map/ppermute | solution.py:53
  29.5 8.2 %copy-start.3 = (f32[256,256]{1,0:T(8,128)}, f32[256,256]{1,0:T(8,128)S(1)}, u32[]{:S(2)}) copy-start(f32[256,256]{1,0:T(8,128)S(1)} %collective-permute-done.2) | copy-start | bytes 786436
  29.5 23.5 %collective-permute-start.1 = (f32[256,1024]{1,0:T(8,128)S(1)}, f32[256,1024]{1,0:T(8,128)}, u32[]{:S(2)}, u32[]{:S(2)}) collective-permute-start(f32[256,1024]{1,0:T(8,128)S(1)} %collective-permute-done.refs_2_), channel_id=1, source_target_pairs={{0,16},{1,17},{2,18},{3,19},{4,20},{5,21},{6,22},{7,23},{8,24},{9,... | collective-permute-start | bytes 3145736 | tf_op jit(solution)/shard_map/ppermute | solution.py:53
  31.1 6.5 %copy-start.4 = (f32[256,256]{1,0:T(8,128)}, f32[256,256]{1,0:T(8,128)S(1)}, u32[]{:S(2)}) copy-start(f32[256,256]{1,0:T(8,128)S(1)} %collective-permute-done.3) | copy-start | bytes 786436
  35.0 15.5 %collective-permute-start.5 = (f32[4,256,256]{2,1,0:T(8,128)}, f32[4,256,256]{2,1,0:T(8,128)}, u32[]{:S(2)}, u32[]{:S(2)}) collective-permute-start(f32[4,256,256]{2,1,0:T(8,128)} %pad_maximum_fusion.1), channel_id=1, source_target_pairs={{0,129},{1,0},{2,131},{3,2},{4,133},{5,4},{6,135},{7,6},{8,137},{9... | collective-permute-start | bytes 3145736 | tf_op jit(solution)/shard_map/ppermute | solution.py:53
  35.5 15.0 %collective-permute-start.6 = (f32[4,256,256]{2,1,0:T(8,128)}, f32[4,256,256]{2,1,0:T(8,128)}, u32[]{:S(2)}, u32[]{:S(2)}) collective-permute-start(f32[4,256,256]{2,1,0:T(8,128)} %pad_maximum_fusion.1), channel_id=1, source_target_pairs={{0,1},{1,128},{2,3},{3,130},{4,5},{5,132},{6,7},{7,134},{8,9},{9,1... | collective-permute-start | bytes 3145736 | tf_op jit(solution)/shard_map/ppermute | solution.py:53
  37.7 22.3 %collective-permute-start.10 = (f32[256,1024]{1,0:T(8,128)S(1)}, f32[256,1024]{1,0:T(8,128)S(1)}, u32[]{:S(2)}, u32[]{:S(2)}) collective-permute-start(f32[256,1024]{1,0:T(8,128)S(1)} %fusion.80.refs_3_), channel_id=1, source_target_pairs={{0,2},{1,3},{2,4},{3,5},{4,6},{5,7},{6,8},{7,9},{8,10},{9,11},{10,... | collective-permute-start | bytes 3145736 | tf_op jit(solution)/shard_map/ppermute | solution.py:53
  40.4 26.4 %collective-permute-start.11 = (f32[256,1024]{1,0:T(8,128)}, f32[256,1024]{1,0:T(8,128)}, u32[]{:S(2)}, u32[]{:S(2)}) collective-permute-start(f32[256,1024]{1,0:T(8,128)} %collective-permute-done.9.refs_4_), channel_id=1, source_target_pairs={{0,14},{1,15},{2,0},{3,1},{4,2},{5,3},{6,4},{7,5},{8,6},{9,7},{10,... | collective-permute-start | bytes 3145736 | tf_op jit(solution)/shard_map/ppermute | solution.py:53
  51.7 19.3 %collective-permute-start.7 = (f32[4,256,256]{2,1,0:T(8,128)}, f32[4,256,256]{2,1,0:T(8,128)S(1)}, u32[]{:S(2)}, u32[]{:S(2)}) collective-permute-start(f32[4,256,256]{2,1,0:T(8,128)} %fusion.82), channel_id=1, source_target_pairs={{0,128},{1,129},{2,130},{3,131},{4,132},{5,133},{6,134},{7,135},{8... | collective-permute-start | bytes 3145736 | tf_op jit(solution)/shard_map/ppermute | solution.py:53
  60.8 31.6 %collective-permute-start.12 = (f32[256,1024]{1,0:T(8,128)S(1)}, f32[256,1024]{1,0:T(8,128)S(1)}, u32[]{:S(2)}, u32[]{:S(2)}) collective-permute-start(f32[256,1024]{1,0:T(8,128)S(1)} %fusion.77.refs_5_), channel_id=1, source_target_pairs={{0,2},{1,3},{2,4},{3,5},{4,6},{5,7},{6,8},{7,9},{8,10},{9,11},{10,... | collective-permute-start | bytes 3145736 | tf_op jit(solution)/shard_map/ppermute | solution.py:53
  66.8 25.4 %collective-permute-start.13 = (f32[256,1024]{1,0:T(8,128)}, f32[256,1024]{1,0:T(8,128)S(1)}, u32[]{:S(2)}, u32[]{:S(2)}) collective-permute-start(f32[256,1024]{1,0:T(8,128)} %collective-permute-done.11.refs_6_), channel_id=1, source_target_pairs={{0,14},{1,15},{2,0},{3,1},{4,2},{5,3},{6,4},{7,5},{8,6},{9,7},{10,... | collective-permute-start | bytes 3145736 | tf_op jit(solution)/shard_map/ppermute | solution.py:53
  92.3 12.9 %collective-permute-start.15 = (f32[128,1024]{1,0:T(8,128)S(1)}, f32[128,1024]{1,0:T(8,128)S(1)}, u32[]{:S(2)}, u32[]{:S(2)}) collective-permute-start(f32[128,1024]{1,0:T(8,128)S(1)} %slice.75), channel_id=1, source_target_pairs={{0,14},{1,15},{2,0},{3,1},{4,2},{5,3},{6,4},{7,5},{8,6},{9,7},{10,... | collective-permute-start | bytes 1572872 | tf_op jit(solution)/shard_map/ppermute | solution.py:53
  92.4 12.8 %collective-permute-start.14 = (f32[128,1024]{1,0:T(8,128)S(1)}, f32[128,1024]{1,0:T(8,128)S(1)}, u32[]{:S(2)}, u32[]{:S(2)}) collective-permute-start(f32[128,1024]{1,0:T(8,128)S(1)} %slice.74), channel_id=1, source_target_pairs={{0,2},{1,3},{2,4},{3,5},{4,6},{5,7},{6,8},{7,9},{8,10},{9,11},{10,... | collective-permute-start | bytes 1572872 | tf_op jit(solution)/shard_map/ppermute | solution.py:53
  106.6 6.7 %collective-permute-start.16 = (f32[512,1024]{1,0:T(8,128)S(1)}, f32[512,1024]{1,0:T(8,128)}, u32[]{:S(2)}, u32[]{:S(2)}) collective-permute-start(f32[512,1024]{1,0:T(8,128)S(1)} %add.281), channel_id=1, source_target_pairs={{0,16},{1,17},{2,18},{3,19},{4,20},{5,21},{6,22},{7,23},{8,24},{9,... | collective-permute-start | bytes 6291464 | tf_op jit(solution)/shard_map/ppermute | solution.py:53
  116.4 7.9 %collective-permute-start.20 = (f32[64,1024]{1,0:T(8,128)S(1)}, f32[64,1024]{1,0:T(8,128)S(1)}, u32[]{:S(2)}, u32[]{:S(2)}) collective-permute-start(f32[64,1024]{1,0:T(8,128)S(1)} %fusion.42), channel_id=1, source_target_pairs={{0,14},{1,15},{2,0},{3,1},{4,2},{5,3},{6,4},{7,5},{8,6},{9,7},{10,... | collective-permute-start | bytes 786440 | tf_op jit(solution)/shard_map/ppermute | solution.py:53
  117.1 8.4 %collective-permute-start.17 = (f32[64,1024]{1,0:T(8,128)S(1)}, f32[64,1024]{1,0:T(8,128)S(1)}, u32[]{:S(2)}, u32[]{:S(2)}) collective-permute-start(f32[64,1024]{1,0:T(8,128)S(1)} %fusion.31), channel_id=1, source_target_pairs={{0,2},{1,3},{2,4},{3,5},{4,6},{5,7},{6,8},{7,9},{8,10},{9,11},{10,... | collective-permute-start | bytes 786440 | tf_op jit(solution)/shard_map/ppermute | solution.py:53
  125.0 7.8 %collective-permute-start.23 = (f32[64,1024]{1,0:T(8,128)S(1)}, f32[64,1024]{1,0:T(8,128)S(1)}, u32[]{:S(2)}, u32[]{:S(2)}) collective-permute-start(f32[64,1024]{1,0:T(8,128)S(1)} %convolution_add_fusion), channel_id=1, source_target_pairs={{0,14},{1,15},{2,0},{3,1},{4,2},{5,3},{6,4},{7,5},{8,6},{9,7},{10,... | collective-permute-start | bytes 786440 | tf_op jit(solution)/shard_map/ppermute | solution.py:53
  126.2 7.6 %collective-permute-start.18 = (f32[64,1024]{1,0:T(8,128)S(1)}, f32[64,1024]{1,0:T(8,128)S(1)}, u32[]{:S(2)}, u32[]{:S(2)}) collective-permute-start(f32[64,1024]{1,0:T(8,128)S(1)} %convolution_add_fusion.1), channel_id=1, source_target_pairs={{0,2},{1,3},{2,4},{3,5},{4,6},{5,7},{6,8},{7,9},{8,10},{9,11},{10,... | collective-permute-start | bytes 786440 | tf_op jit(solution)/shard_map/ppermute | solution.py:53
  128.5 19.6 %collective-permute-start.21 = (f32[256,1024]{1,0:T(8,128)S(1)}, f32[256,1024]{1,0:T(8,128)S(1)}, u32[]{:S(2)}, u32[]{:S(2)}) collective-permute-start(f32[256,1024]{1,0:T(8,128)S(1)} %constant_dynamic-slice_fusion), channel_id=1, source_target_pairs={{0,0},{1,16},{2,2},{3,18},{4,4},{5,20},{6,6},{7,22},{8,8},{9,24},{... | collective-permute-start | bytes 3145736 | tf_op jit(solution)/shard_map/ppermute | solution.py:53
  133.4 6.7 %collective-permute-start.24 = (f32[64,1024]{1,0:T(8,128)S(1)}, f32[64,1024]{1,0:T(8,128)S(1)}, u32[]{:S(2)}, u32[]{:S(2)}) collective-permute-start(f32[64,1024]{1,0:T(8,128)S(1)} %fusion.59), channel_id=1, source_target_pairs={{0,14},{1,15},{2,0},{3,1},{4,2},{5,3},{6,4},{7,5},{8,6},{9,7},{10,... | collective-permute-start | bytes 786440 | tf_op jit(solution)/shard_map/ppermute | solution.py:53
  134.5 12.9 %collective-permute-start.19 = (f32[64,1024]{1,0:T(8,128)S(1)}, f32[64,1024]{1,0:T(8,128)S(1)}, u32[]{:S(2)}, u32[]{:S(2)}) collective-permute-start(f32[64,1024]{1,0:T(8,128)S(1)} %fusion.19), channel_id=1, source_target_pairs={{0,2},{1,3},{2,4},{3,5},{4,6},{5,7},{6,8},{7,9},{8,10},{9,11},{10,... | collective-permute-start | bytes 786440 | tf_op jit(solution)/shard_map/ppermute | solution.py:53
  140.9 12.6 %collective-permute-start.25 = (f32[64,1024]{1,0:T(8,128)S(1)}, f32[64,1024]{1,0:T(8,128)S(1)}, u32[]{:S(2)}, u32[]{:S(2)}) collective-permute-start(f32[64,1024]{1,0:T(8,128)S(1)} %fusion.50), channel_id=1, source_target_pairs={{0,0},{1,16},{2,2},{3,18},{4,4},{5,20},{6,6},{7,22},{8,8},{9,24},{... | collective-permute-start | bytes 786440 | tf_op jit(solution)/shard_map/ppermute | solution.py:53
  147.4 4.0 %copy-start.1 = (f32[32,8,4,256]{3,1,2,0:T(8,128)S(1)}, f32[32,8,4,256]{3,1,2,0:T(8,128)}, u32[]{:S(2)}) copy-start(f32[32,8,4,256]{3,1,2,0:T(8,128)} %copy-done) | copy-start | bytes 3145732
  148.1 8.0 %copy-start.7 = (f32[64,1024]{1,0:T(8,128)S(1)}, f32[64,1024]{1,0:T(8,128)}, u32[]{:S(2)}) copy-start(f32[64,1024]{1,0:T(8,128)} %param.9) | copy-start | bytes 786436
  148.1 8.0 %collective-permute-start.22 = (f32[64,1024]{1,0:T(8,128)S(1)}, f32[64,1024]{1,0:T(8,128)S(1)}, u32[]{:S(2)}, u32[]{:S(2)}) collective-permute-start(f32[64,1024]{1,0:T(8,128)S(1)} %fusion.10), channel_id=1, source_target_pairs={{0,2},{1,18},{2,4},{3,20},{4,6},{5,22},{6,8},{7,24},{8,10},{9,26},... | collective-permute-start | bytes 786440 | tf_op jit(solution)/shard_map/ppermute | solution.py:53
  (3 other events, 8.2 us)

commit v4 on v3

--- a/solution.py
+++ b/solution.py
@@ -139,10 +139,10 @@
     astern = [own, send(own, ring(-1))]
     beside = [send(line, along_plane(-1, 1)), None, send(line, along_plane(-3, 1))]
     other = send(own, swap_cores())
-    ahead.append(after(send(ahead[1], ring(1)), beside[0::2] + [other]))
+    ahead.append(after(send(ahead[1], ring(1)), beside[0::2]))
     astern.append(send(astern[1], ring(-1)))
     beside[1] = send(after(line, beside[0::2]), along_plane(-2, 1))
-    ahead.append(after(send(ahead[2], ring(1)), beside[1:2]))
+    ahead.append(after(send(ahead[2], ring(1)), beside[1:2] + [other]))
     astern.append(send(astern[2], ring(-1)))
     near = jnp.concatenate([line] + beside)
 

time: 157 us -> 157 us (level)
  starting transfers between devices: 50.9 us -> 53.8 us
  waiting for transfers between devices: 71.8 us -> 68.9 us
    ppermute x26, waiting for transfers between devices: 71.8 us -> 68.9 us  [send(): return lax.ppermute(value, AXES, perm)]
    ppermute x26, starting transfers between devices: 50.9 us -> 53.8 us  [send(): return lax.ppermute(value, AXES, perm)]
    unnamed x25 -> x27, local copies, waits for them, and re-layouts: 4.57 us -> 4.57 us
where the time goes in v4:
time: 157 us
  waiting for transfers between devices  68.9 us (44%)
  starting transfers between devices  53.8 us (34%)
  other arithmetic  11.2 us (7%)
  Pallas kernels  8.98 us (6%)
  matrix products  6.57 us (4%)
  local copies, waits for them, and re-layouts  6.45 us (4%)
    ppermute x26, waiting for transfers between devices, send(): return lax.ppermute(value, AXES, perm)  68.9 us
    ppermute x26, starting transfers between devices, send(): return lax.ppermute(value, AXES, perm)  53.8 us
    pallas_call x1, Pallas kernels, products(): pl.pallas_call(lambda *refs: product_kernel(count, *refs), grid_spec=pltp...  8.98 us
    dot_general x8, matrix products, term(): return jnp.dot(joined, right, preferred_element_type=jnp.float32)  5.53 us
    unnamed x27, local copies, waits for them, and re-layouts  4.57 us
  transfers between devices with their start and end apart: 26, of which 15 were waited for; matrix products, arithmetic and copies ran while one was open for 11% of the time, Pallas kernels for 6%

profile of v4, /device:TPU:25, one launch (start us, length us, event | category | flops | bytes accessed | tf_op | source)
XLA Modules:
  0.0 156.9 jit_solution(17861708302425670046)
XLA Ops:
  2.1 3.7 %collective-permute-start = (f32[256,1024]{1,0:T(8,128)S(1)}, f32[256,1024]{1,0:T(8,128)S(1)}, u32[]{:S(2)}, u32[]{:S(2)}) collective-permute-start(f32[256,1024]{1,0:T(8,128)S(1)} %mul.179), channel_id=1, source_target_pairs={{0,0},{1,16},{2,2},{3,18},{4,4},{5,20},{6,6},{7,22},{8,8},{9,24},{... | collective-permute-start | bytes 3145736 | tf_op jit(solution)/shard_map/ppermute | solution.py:53
  5.7 12.9 %collective-permute-done.refs_2_ = f32[256,1024]{1,0:T(8,128)S(1)} collective-permute-done((f32[256,1024]{1,0:T(8,128)S(1)}, f32[256,1024]{1,0:T(8,128)S(1)}, u32[]{:S(2)}, u32[]{:S(2)}) %collective-permute-start) | collective-permute-done | bytes 1048608 | tf_op jit(solution)/shard_map/ppermute | solution.py:53
  18.6 5.6 %collective-permute-start.8 = (f32[256,1024]{1,0:T(8,128)S(1)}, f32[256,1024]{1,0:T(8,128)S(1)}, u32[]{:S(2)}, u32[]{:S(2)}) collective-permute-start(f32[256,1024]{1,0:T(8,128)S(1)} %collective-permute-done.refs_2_), channel_id=1, source_target_pairs={{0,2},{1,3},{2,4},{3,5},{4,6},{5,7},{6,8},{7,9},{8,10},{9,11},{10,... | collective-permute-start | bytes 3145736 | tf_op jit(solution)/shard_map/ppermute | solution.py:53
  24.3 2.8 %collective-permute-start.3 = (f32[256,256]{1,0:T(8,128)S(1)}, f32[256,256]{1,0:T(8,128)S(1)}, u32[]{:S(2)}, u32[]{:S(2)}) collective-permute-start(f32[256,256]{1,0:T(8,128)S(1)} %fusion.83), channel_id=1, source_target_pairs={{0,64},{1,65},{2,66},{3,67},{4,68},{5,69},{6,70},{7,71},{8,72},{9,... | collective-permute-start | bytes 786440 | tf_op jit(solution)/shard_map/ppermute | solution.py:53
  27.8 1.7 %collective-permute-done.2 = f32[256,256]{1,0:T(8,128)S(1)} collective-permute-done((f32[256,256]{1,0:T(8,128)S(1)}, f32[256,256]{1,0:T(8,128)S(1)}, u32[]{:S(2)}, u32[]{:S(2)}) %collective-permute-start.2) | collective-permute-done | bytes 262176 | tf_op jit(solution)/shard_map/ppermute | solution.py:53
  29.5 1.6 %collective-permute-done.3 = f32[256,256]{1,0:T(8,128)S(1)} collective-permute-done((f32[256,256]{1,0:T(8,128)S(1)}, f32[256,256]{1,0:T(8,128)S(1)}, u32[]{:S(2)}, u32[]{:S(2)}) %collective-permute-start.3) | collective-permute-done | bytes 262176 | tf_op jit(solution)/shard_map/ppermute | solution.py:53
  31.1 2.8 %collective-permute-done.4 = f32[256,256]{1,0:T(8,128)S(1)} collective-permute-done((f32[256,256]{1,0:T(8,128)S(1)}, f32[256,256]{1,0:T(8,128)S(1)}, u32[]{:S(2)}, u32[]{:S(2)}) %collective-permute-start.4) | collective-permute-done | bytes 262176 | tf_op jit(solution)/shard_map/ppermute | solution.py:53
  35.5 2.2 %collective-permute-start.6 = (f32[4,256,256]{2,1,0:T(8,128)}, f32[4,256,256]{2,1,0:T(8,128)}, u32[]{:S(2)}, u32[]{:S(2)}) collective-permute-start(f32[4,256,256]{2,1,0:T(8,128)} %pad_maximum_fusion.1), channel_id=1, source_target_pairs={{0,1},{1,128},{2,3},{3,130},{4,5},{5,132},{6,7},{7,134},{8,9},{9,1... | collective-permute-start | bytes 3145736 | tf_op jit(solution)/shard_map/ppermute | solution.py:53
  37.7 2.7 %collective-permute-start.10 = (f32[256,1024]{1,0:T(8,128)S(1)}, f32[256,1024]{1,0:T(8,128)S(1)}, u32[]{:S(2)}, u32[]{:S(2)}) collective-permute-start(f32[256,1024]{1,0:T(8,128)S(1)} %fusion.80.refs_3_), channel_id=1, source_target_pairs={{0,2},{1,3},{2,4},{3,5},{4,6},{5,7},{6,8},{7,9},{8,10},{9,11},{10,... | collective-permute-start | bytes 3145736 | tf_op jit(solution)/shard_map/ppermute | solution.py:53
  40.5 2.9 %collective-permute-start.1 = (f32[256,1024]{1,0:T(8,128)S(1)}, f32[256,1024]{1,0:T(8,128)S(1)}, u32[]{:S(2)}, u32[]{:S(2)}) collective-permute-start(f32[256,1024]{1,0:T(8,128)S(1)} %collective-permute-done.refs_2_), channel_id=1, source_target_pairs={{0,16},{1,17},{2,18},{3,19},{4,20},{5,21},{6,22},{7,23},{8,24},{9,... | collective-permute-start | bytes 3145736 | tf_op jit(solution)/shard_map/ppermute | solution.py:53
  43.4 7.1 %collective-permute-done.5 = f32[4,256,256]{2,1,0:T(8,128)} collective-permute-done((f32[4,256,256]{2,1,0:T(8,128)}, f32[4,256,256]{2,1,0:T(8,128)}, u32[]{:S(2)}, u32[]{:S(2)}) %collective-permute-start.5) | collective-permute-done | bytes 1048608 | tf_op jit(solution)/shard_map/ppermute | solution.py:53
  53.0 7.1 %collective-permute-done.10 = f32[256,1024]{1,0:T(8,128)S(1)} collective-permute-done((f32[256,1024]{1,0:T(8,128)S(1)}, f32[256,1024]{1,0:T(8,128)S(1)}, u32[]{:S(2)}, u32[]{:S(2)}) %collective-permute-start.10) | collective-permute-done | bytes 1048608 | tf_op jit(solution)/shard_map/ppermute | solution.py:53
  60.8 3.5 %collective-permute-start.12 = (f32[256,1024]{1,0:T(8,128)S(1)}, f32[256,1024]{1,0:T(8,128)S(1)}, u32[]{:S(2)}, u32[]{:S(2)}) collective-permute-start(f32[256,1024]{1,0:T(8,128)S(1)} %fusion.77.refs_5_), channel_id=1, source_target_pairs={{0,2},{1,3},{2,4},{3,5},{4,6},{5,7},{6,8},{7,9},{8,10},{9,11},{10,... | collective-permute-start | bytes 3145736 | tf_op jit(solution)/shard_map/ppermute | solution.py:53
  64.3 2.6 %collective-permute-done.11.refs_6_ = f32[256,1024]{1,0:T(8,128)} collective-permute-done((f32[256,1024]{1,0:T(8,128)}, f32[256,1024]{1,0:T(8,128)}, u32[]{:S(2)}, u32[]{:S(2)}) %collective-permute-start.11) | collective-permute-done | bytes 1048608 | tf_op jit(solution)/shard_map/ppermute | solution.py:53
  69.8 1.3 constant_dynamic-update-slice_fusion.2
  71.2 1.3 constant_dynamic-update-slice_fusion.refs_1_
  72.5 19.7 %collective-permute-done.13.refs_8_ = f32[256,1024]{1,0:T(8,128)S(1)} collective-permute-done((f32[256,1024]{1,0:T(8,128)}, f32[256,1024]{1,0:T(8,128)S(1)}, u32[]{:S(2)}, u32[]{:S(2)}) %collective-permute-start.13) | collective-permute-done | bytes 1048608 | tf_op jit(solution)/shard_map/ppermute | solution.py:53
  92.5 2.9 %collective-permute-start.14 = (f32[128,1024]{1,0:T(8,128)S(1)}, f32[128,1024]{1,0:T(8,128)S(1)}, u32[]{:S(2)}, u32[]{:S(2)}) collective-permute-start(f32[128,1024]{1,0:T(8,128)S(1)} %slice.74), channel_id=1, source_target_pairs={{0,2},{1,3},{2,4},{3,5},{4,6},{5,7},{6,8},{7,9},{8,10},{9,11},{10,... | collective-permute-start | bytes 1572872 | tf_op jit(solution)/shard_map/ppermute | solution.py:53
  95.4 9.0 %shard_map.68 = f32[512,1024]{1,0:T(8,128)S(1)} custom-call(s32[14]{0:T(128)S(1)} %stack.74.refs_0_, f32[16,256,256]{2,1,0:T(8,128)S(1)} %constant_dynamic-update-slice_fusion.refs_1_, f32[256,1024]{1,0:T(8,128)S(1)} %collective-permute-done.refs_2_, f32[256,1024]{1,0:T(8,128)S(1)} %fusion.80.refs_3_, f32[256,1024]{1,0:T(8,128)} %collective-permute-done.9.refs_4_, ...), custom_call_target="tpu_custom_call" | custom-call | flops 5637144576 | bytes 13631488 | tf_op jit(solution)/shard_map/pallas_call | solution.py:94
  106.7 2.8 %collective-permute-start.16 = (f32[512,1024]{1,0:T(8,128)S(1)}, f32[512,1024]{1,0:T(8,128)}, u32[]{:S(2)}, u32[]{:S(2)}) collective-permute-start(f32[512,1024]{1,0:T(8,128)S(1)} %add.281), channel_id=1, source_target_pairs={{0,16},{1,17},{2,18},{3,19},{4,20},{5,21},{6,22},{7,23},{8,24},{9,... | collective-permute-start | bytes 6291464 | tf_op jit(solution)/shard_map/ppermute | solution.py:53
  109.5 1.8 %maximum_select_fusion = f32[512,1024]{1,0:T(8,128)S(1)} fusion(f32[256,1024]{1,0:T(8,128)} %copy-done.6, f32[256,1024]{1,0:T(8,128)S(1)} %collective-permute-done.refs_2_, pred[]{:T(512)S(6)} %eq.8), kind=kLoop, calls=%fused_computation.4 | loop fusion | flops 1572864 | bytes 4194305 | tf_op jit(solution)/shard_map/jit(_where)/select_n | solution.py:156
  112.1 1.3 collective-permute-done.16
  113.4 2.1 %fusion = (bf16[512,1024]{1,0:T(8,128)(2,1)S(1)}, f32[512,1024]{1,0:T(8,128)S(1)}) fusion(f32[512,1024]{1,0:T(8,128)S(1)} %add.281, f32[512,1024]{1,0:T(8,128)} %collective-permute-done.16), kind=kLoop, calls=%fused_computation.3 | loop fusion | flops 2097152 | bytes 7340032 | tf_op jit(solution)/shard_map/convert_element_type | solution.py:177
  117.2 2.7 %collective-permute-start.17 = (f32[64,1024]{1,0:T(8,128)S(1)}, f32[64,1024]{1,0:T(8,128)S(1)}, u32[]{:S(2)}, u32[]{:S(2)}) collective-permute-start(f32[64,1024]{1,0:T(8,128)S(1)} %fusion.31), channel_id=1, source_target_pairs={{0,2},{1,3},{2,4},{3,5},{4,6},{5,7},{6,8},{7,9},{8,10},{9,11},{10,... | collective-permute-start | bytes 786440 | tf_op jit(solution)/shard_map/ppermute | solution.py:53
  120.0 4.3 %collective-permute-done.20 = f32[64,1024]{1,0:T(8,128)S(1)} collective-permute-done((f32[64,1024]{1,0:T(8,128)S(1)}, f32[64,1024]{1,0:T(8,128)S(1)}, u32[]{:S(2)}, u32[]{:S(2)}) %collective-permute-start.20) | collective-permute-done | bytes 262176 | tf_op jit(solution)/shard_map/ppermute | solution.py:53
  126.2 2.3 %collective-permute-start.18 = (f32[64,1024]{1,0:T(8,128)S(1)}, f32[64,1024]{1,0:T(8,128)S(1)}, u32[]{:S(2)}, u32[]{:S(2)}) collective-permute-start(f32[64,1024]{1,0:T(8,128)S(1)} %convolution_add_fusion.1), channel_id=1, source_target_pairs={{0,2},{1,3},{2,4},{3,5},{4,6},{5,7},{6,8},{7,9},{8,10},{9,11},{10,... | collective-permute-start | bytes 786440 | tf_op jit(solution)/shard_map/ppermute | solution.py:53
  128.5 4.2 %collective-permute-start.21 = (f32[256,1024]{1,0:T(8,128)S(1)}, f32[256,1024]{1,0:T(8,128)S(1)}, u32[]{:S(2)}, u32[]{:S(2)}) collective-permute-start(f32[256,1024]{1,0:T(8,128)S(1)} %constant_dynamic-slice_fusion), channel_id=1, source_target_pairs={{0,0},{1,16},{2,2},{3,18},{4,4},{5,20},{6,6},{7,22},{8,8},{9,24},{... | collective-permute-start | bytes 3145736 | tf_op jit(solution)/shard_map/ppermute | solution.py:53
  134.5 2.7 %collective-permute-start.19 = (f32[64,1024]{1,0:T(8,128)S(1)}, f32[64,1024]{1,0:T(8,128)S(1)}, u32[]{:S(2)}, u32[]{:S(2)}) collective-permute-start(f32[64,1024]{1,0:T(8,128)S(1)} %fusion.19), channel_id=1, source_target_pairs={{0,2},{1,3},{2,4},{3,5},{4,6},{5,7},{6,8},{7,9},{8,10},{9,11},{10,... | collective-permute-start | bytes 786440 | tf_op jit(solution)/shard_map/ppermute | solution.py:53
  137.2 3.0 %collective-permute-done.24 = f32[64,1024]{1,0:T(8,128)S(1)} collective-permute-done((f32[64,1024]{1,0:T(8,128)S(1)}, f32[64,1024]{1,0:T(8,128)S(1)}, u32[]{:S(2)}, u32[]{:S(2)}) %collective-permute-start.24) | collective-permute-done | bytes 262176 | tf_op jit(solution)/shard_map/ppermute | solution.py:53
  140.9 6.5 %collective-permute-start.25 = (f32[64,1024]{1,0:T(8,128)S(1)}, f32[64,1024]{1,0:T(8,128)S(1)}, u32[]{:S(2)}, u32[]{:S(2)}) collective-permute-start(f32[64,1024]{1,0:T(8,128)S(1)} %fusion.50), channel_id=1, source_target_pairs={{0,0},{1,16},{2,2},{3,18},{4,4},{5,20},{6,6},{7,22},{8,8},{9,24},{... | collective-permute-start | bytes 786440 | tf_op jit(solution)/shard_map/ppermute | solution.py:53
  148.1 3.2 %collective-permute-start.22 = (f32[64,1024]{1,0:T(8,128)S(1)}, f32[64,1024]{1,0:T(8,128)S(1)}, u32[]{:S(2)}, u32[]{:S(2)}) collective-permute-start(f32[64,1024]{1,0:T(8,128)S(1)} %fusion.10), channel_id=1, source_target_pairs={{0,2},{1,18},{2,4},{3,20},{4,6},{5,22},{6,8},{7,24},{8,10},{9,26},... | collective-permute-start | bytes 786440 | tf_op jit(solution)/shard_map/ppermute | solution.py:53
  153.5 2.6 %collective-permute-done.22 = f32[64,1024]{1,0:T(8,128)S(1)} collective-permute-done((f32[64,1024]{1,0:T(8,128)S(1)}, f32[64,1024]{1,0:T(8,128)S(1)}, u32[]{:S(2)}, u32[]{:S(2)}) %collective-permute-start.22) | collective-permute-done | bytes 262176 | tf_op jit(solution)/shard_map/ppermute | solution.py:53
  (80 shorter events, 23.0 us)
Async XLA Ops:
  1.4 22.8 %copy-start.2 = (f32[256,256]{1,0:T(8,128)S(1)}, f32[256,256]{1,0:T(8,128)}, u32[]{:S(2)}) copy-start(f32[256,256]{1,0:T(8,128)} %param.5) | copy-start | bytes 786436
  1.8 16.8 %copy-start = (f32[32,8,4,256]{3,1,2,0:T(8,128)}, f32[32,8,4,256]{3,1,2,0:T(8,128)S(1)}, u32[]{:S(2)}) copy-start(f32[32,8,4,256]{3,1,2,0:T(8,128)S(1)} %copy.7) | copy-start | bytes 3145732
  2.1 16.6 %collective-permute-start = (f32[256,1024]{1,0:T(8,128)S(1)}, f32[256,1024]{1,0:T(8,128)S(1)}, u32[]{:S(2)}, u32[]{:S(2)}) collective-permute-start(f32[256,1024]{1,0:T(8,128)S(1)} %mul.179), channel_id=1, source_target_pairs={{0,0},{1,16},{2,2},{3,18},{4,4},{5,20},{6,6},{7,22},{8,8},{9,24},{... | collective-permute-start | bytes 3145736 | tf_op jit(solution)/shard_map/ppermute | solution.py:53
  18.6 19.1 %collective-permute-start.8 = (f32[256,1024]{1,0:T(8,128)S(1)}, f32[256,1024]{1,0:T(8,128)S(1)}, u32[]{:S(2)}, u32[]{:S(2)}) collective-permute-start(f32[256,1024]{1,0:T(8,128)S(1)} %collective-permute-done.refs_2_), channel_id=1, source_target_pairs={{0,2},{1,3},{2,4},{3,5},{4,6},{5,7},{6,8},{7,9},{8,10},{9,11},{10,... | collective-permute-start | bytes 3145736 | tf_op jit(solution)/shard_map/ppermute | solution.py:53
  24.2 16.2 %collective-permute-start.9 = (f32[256,1024]{1,0:T(8,128)S(1)}, f32[256,1024]{1,0:T(8,128)}, u32[]{:S(2)}, u32[]{:S(2)}) collective-permute-start(f32[256,1024]{1,0:T(8,128)S(1)} %collective-permute-done.refs_2_), channel_id=1, source_target_pairs={{0,14},{1,15},{2,0},{3,1},{4,2},{5,3},{6,4},{7,5},{8,6},{9,7},{10,... | collective-permute-start | bytes 3145736 | tf_op jit(solution)/shard_map/ppermute | solution.py:53
  24.2 5.3 %collective-permute-start.2 = (f32[256,256]{1,0:T(8,128)S(1)}, f32[256,256]{1,0:T(8,128)S(1)}, u32[]{:S(2)}, u32[]{:S(2)}) collective-permute-start(f32[256,256]{1,0:T(8,128)S(1)} %fusion.83), channel_id=1, source_target_pairs={{0,96},{1,97},{2,98},{3,99},{4,100},{5,101},{6,102},{7,103},{8,104... | collective-permute-start | bytes 786440 | tf_op jit(solution)/shard_map/ppermute | solution.py:53
  24.3 6.9 %collective-permute-start.3 = (f32[256,256]{1,0:T(8,128)S(1)}, f32[256,256]{1,0:T(8,128)S(1)}, u32[]{:S(2)}, u32[]{:S(2)}) collective-permute-start(f32[256,256]{1,0:T(8,128)S(1)} %fusion.83), channel_id=1, source_target_pairs={{0,64},{1,65},{2,66},{3,67},{4,68},{5,69},{6,70},{7,71},{8,72},{9,... | collective-permute-start | bytes 786440 | tf_op jit(solution)/shard_map/ppermute | solution.py:53
  27.1 6.8 %collective-permute-start.4 = (f32[256,256]{1,0:T(8,128)S(1)}, f32[256,256]{1,0:T(8,128)S(1)}, u32[]{:S(2)}, u32[]{:S(2)}) collective-permute-start(f32[256,256]{1,0:T(8,128)S(1)} %fusion.83), channel_id=1, source_target_pairs={{0,32},{1,33},{2,34},{3,35},{4,36},{5,37},{6,38},{7,39},{8,40},{9,... | collective-permute-start | bytes 786440 | tf_op jit(solution)/shard_map/ppermute | solution.py:53
  29.5 8.2 %copy-start.3 = (f32[256,256]{1,0:T(8,128)}, f32[256,256]{1,0:T(8,128)S(1)}, u32[]{:S(2)}) copy-start(f32[256,256]{1,0:T(8,128)S(1)} %collective-permute-done.2) | copy-start | bytes 786436
  31.1 6.6 %copy-start.4 = (f32[256,256]{1,0:T(8,128)}, f32[256,256]{1,0:T(8,128)S(1)}, u32[]{:S(2)}) copy-start(f32[256,256]{1,0:T(8,128)S(1)} %collective-permute-done.3) | copy-start | bytes 786436
  35.0 15.5 %collective-permute-start.5 = (f32[4,256,256]{2,1,0:T(8,128)}, f32[4,256,256]{2,1,0:T(8,128)}, u32[]{:S(2)}, u32[]{:S(2)}) collective-permute-start(f32[4,256,256]{2,1,0:T(8,128)} %pad_maximum_fusion.1), channel_id=1, source_target_pairs={{0,129},{1,0},{2,131},{3,2},{4,133},{5,4},{6,135},{7,6},{8,137},{9... | collective-permute-start | bytes 3145736 | tf_op jit(solution)/shard_map/ppermute | solution.py:53
  35.5 15.0 %collective-permute-start.6 = (f32[4,256,256]{2,1,0:T(8,128)}, f32[4,256,256]{2,1,0:T(8,128)}, u32[]{:S(2)}, u32[]{:S(2)}) collective-permute-start(f32[4,256,256]{2,1,0:T(8,128)} %pad_maximum_fusion.1), channel_id=1, source_target_pairs={{0,1},{1,128},{2,3},{3,130},{4,5},{5,132},{6,7},{7,134},{8,9},{9,1... | collective-permute-start | bytes 3145736 | tf_op jit(solution)/shard_map/ppermute | solution.py:53
  37.7 22.3 %collective-permute-start.10 = (f32[256,1024]{1,0:T(8,128)S(1)}, f32[256,1024]{1,0:T(8,128)S(1)}, u32[]{:S(2)}, u32[]{:S(2)}) collective-permute-start(f32[256,1024]{1,0:T(8,128)S(1)} %fusion.80.refs_3_), channel_id=1, source_target_pairs={{0,2},{1,3},{2,4},{3,5},{4,6},{5,7},{6,8},{7,9},{8,10},{9,11},{10,... | collective-permute-start | bytes 3145736 | tf_op jit(solution)/shard_map/ppermute | solution.py:53
  40.4 26.4 %collective-permute-start.11 = (f32[256,1024]{1,0:T(8,128)}, f32[256,1024]{1,0:T(8,128)}, u32[]{:S(2)}, u32[]{:S(2)}) collective-permute-start(f32[256,1024]{1,0:T(8,128)} %collective-permute-done.9.refs_4_), channel_id=1, source_target_pairs={{0,14},{1,15},{2,0},{3,1},{4,2},{5,3},{6,4},{7,5},{8,6},{9,7},{10,... | collective-permute-start | bytes 3145736 | tf_op jit(solution)/shard_map/ppermute | solution.py:53
  40.5 51.9 %collective-permute-start.1 = (f32[256,1024]{1,0:T(8,128)S(1)}, f32[256,1024]{1,0:T(8,128)S(1)}, u32[]{:S(2)}, u32[]{:S(2)}) collective-permute-start(f32[256,1024]{1,0:T(8,128)S(1)} %collective-permute-done.refs_2_), channel_id=1, source_target_pairs={{0,16},{1,17},{2,18},{3,19},{4,20},{5,21},{6,22},{7,23},{8,24},{9,... | collective-permute-start | bytes 3145736 | tf_op jit(solution)/shard_map/ppermute | solution.py:53
  51.8 19.3 %collective-permute-start.7 = (f32[4,256,256]{2,1,0:T(8,128)}, f32[4,256,256]{2,1,0:T(8,128)S(1)}, u32[]{:S(2)}, u32[]{:S(2)}) collective-permute-start(f32[4,256,256]{2,1,0:T(8,128)} %fusion.82), channel_id=1, source_target_pairs={{0,128},{1,129},{2,130},{3,131},{4,132},{5,133},{6,134},{7,135},{8... | collective-permute-start | bytes 3145736 | tf_op jit(solution)/shard_map/ppermute | solution.py:53
  60.8 31.6 %collective-permute-start.12 = (f32[256,1024]{1,0:T(8,128)S(1)}, f32[256,1024]{1,0:T(8,128)S(1)}, u32[]{:S(2)}, u32[]{:S(2)}) collective-permute-start(f32[256,1024]{1,0:T(8,128)S(1)} %fusion.77.refs_5_), channel_id=1, source_target_pairs={{0,2},{1,3},{2,4},{3,5},{4,6},{5,7},{6,8},{7,9},{8,10},{9,11},{10,... | collective-permute-start | bytes 3145736 | tf_op jit(solution)/shard_map/ppermute | solution.py:53
  66.8 25.4 %collective-permute-start.13 = (f32[256,1024]{1,0:T(8,128)}, f32[256,1024]{1,0:T(8,128)S(1)}, u32[]{:S(2)}, u32[]{:S(2)}) collective-permute-start(f32[256,1024]{1,0:T(8,128)} %collective-permute-done.11.refs_6_), channel_id=1, source_target_pairs={{0,14},{1,15},{2,0},{3,1},{4,2},{5,3},{6,4},{7,5},{8,6},{9,7},{10,... | collective-permute-start | bytes 3145736 | tf_op jit(solution)/shard_map/ppermute | solution.py:53
  92.3 12.9 %collective-permute-start.15 = (f32[128,1024]{1,0:T(8,128)S(1)}, f32[128,1024]{1,0:T(8,128)S(1)}, u32[]{:S(2)}, u32[]{:S(2)}) collective-permute-start(f32[128,1024]{1,0:T(8,128)S(1)} %slice.75), channel_id=1, source_target_pairs={{0,14},{1,15},{2,0},{3,1},{4,2},{5,3},{6,4},{7,5},{8,6},{9,7},{10,... | collective-permute-start | bytes 1572872 | tf_op jit(solution)/shard_map/ppermute | solution.py:53
  92.4 12.0 %copy-start.6 = (f32[256,1024]{1,0:T(8,128)}, f32[256,1024]{1,0:T(8,128)S(1)}, u32[]{:S(2)}) copy-start(f32[256,1024]{1,0:T(8,128)S(1)} %collective-permute-done.1) | copy-start | bytes 3145732
  92.5 12.7 %collective-permute-start.14 = (f32[128,1024]{1,0:T(8,128)S(1)}, f32[128,1024]{1,0:T(8,128)S(1)}, u32[]{:S(2)}, u32[]{:S(2)}) collective-permute-start(f32[128,1024]{1,0:T(8,128)S(1)} %slice.74), channel_id=1, source_target_pairs={{0,2},{1,3},{2,4},{3,5},{4,6},{5,7},{6,8},{7,9},{8,10},{9,11},{10,... | collective-permute-start | bytes 1572872 | tf_op jit(solution)/shard_map/ppermute | solution.py:53
  106.7 6.7 %collective-permute-start.16 = (f32[512,1024]{1,0:T(8,128)S(1)}, f32[512,1024]{1,0:T(8,128)}, u32[]{:S(2)}, u32[]{:S(2)}) collective-permute-start(f32[512,1024]{1,0:T(8,128)S(1)} %add.281), channel_id=1, source_target_pairs={{0,16},{1,17},{2,18},{3,19},{4,20},{5,21},{6,22},{7,23},{8,24},{9,... | collective-permute-start | bytes 6291464 | tf_op jit(solution)/shard_map/ppermute | solution.py:53
  116.4 7.9 %collective-permute-start.20 = (f32[64,1024]{1,0:T(8,128)S(1)}, f32[64,1024]{1,0:T(8,128)S(1)}, u32[]{:S(2)}, u32[]{:S(2)}) collective-permute-start(f32[64,1024]{1,0:T(8,128)S(1)} %fusion.42), channel_id=1, source_target_pairs={{0,14},{1,15},{2,0},{3,1},{4,2},{5,3},{6,4},{7,5},{8,6},{9,7},{10,... | collective-permute-start | bytes 786440 | tf_op jit(solution)/shard_map/ppermute | solution.py:53
  117.2 8.4 %collective-permute-start.17 = (f32[64,1024]{1,0:T(8,128)S(1)}, f32[64,1024]{1,0:T(8,128)S(1)}, u32[]{:S(2)}, u32[]{:S(2)}) collective-permute-start(f32[64,1024]{1,0:T(8,128)S(1)} %fusion.31), channel_id=1, source_target_pairs={{0,2},{1,3},{2,4},{3,5},{4,6},{5,7},{6,8},{7,9},{8,10},{9,11},{10,... | collective-permute-start | bytes 786440 | tf_op jit(solution)/shard_map/ppermute | solution.py:53
  125.0 7.7 %collective-permute-start.23 = (f32[64,1024]{1,0:T(8,128)S(1)}, f32[64,1024]{1,0:T(8,128)S(1)}, u32[]{:S(2)}, u32[]{:S(2)}) collective-permute-start(f32[64,1024]{1,0:T(8,128)S(1)} %convolution_add_fusion), channel_id=1, source_target_pairs={{0,14},{1,15},{2,0},{3,1},{4,2},{5,3},{6,4},{7,5},{8,6},{9,7},{10,... | collective-permute-start | bytes 786440 | tf_op jit(solution)/shard_map/ppermute | solution.py:53
  126.2 7.5 %collective-permute-start.18 = (f32[64,1024]{1,0:T(8,128)S(1)}, f32[64,1024]{1,0:T(8,128)S(1)}, u32[]{:S(2)}, u32[]{:S(2)}) collective-permute-start(f32[64,1024]{1,0:T(8,128)S(1)} %convolution_add_fusion.1), channel_id=1, source_target_pairs={{0,2},{1,3},{2,4},{3,5},{4,6},{5,7},{6,8},{7,9},{8,10},{9,11},{10,... | collective-permute-start | bytes 786440 | tf_op jit(solution)/shard_map/ppermute | solution.py:53
  128.5 19.6 %collective-permute-start.21 = (f32[256,1024]{1,0:T(8,128)S(1)}, f32[256,1024]{1,0:T(8,128)S(1)}, u32[]{:S(2)}, u32[]{:S(2)}) collective-permute-start(f32[256,1024]{1,0:T(8,128)S(1)} %constant_dynamic-slice_fusion), channel_id=1, source_target_pairs={{0,0},{1,16},{2,2},{3,18},{4,4},{5,20},{6,6},{7,22},{8,8},{9,24},{... | collective-permute-start | bytes 3145736 | tf_op jit(solution)/shard_map/ppermute | solution.py:53
  133.5 6.7 %collective-permute-start.24 = (f32[64,1024]{1,0:T(8,128)S(1)}, f32[64,1024]{1,0:T(8,128)S(1)}, u32[]{:S(2)}, u32[]{:S(2)}) collective-permute-start(f32[64,1024]{1,0:T(8,128)S(1)} %fusion.59), channel_id=1, source_target_pairs={{0,14},{1,15},{2,0},{3,1},{4,2},{5,3},{6,4},{7,5},{8,6},{9,7},{10,... | collective-permute-start | bytes 786440 | tf_op jit(solution)/shard_map/ppermute | solution.py:53
  134.5 12.9 %collective-permute-start.19 = (f32[64,1024]{1,0:T(8,128)S(1)}, f32[64,1024]{1,0:T(8,128)S(1)}, u32[]{:S(2)}, u32[]{:S(2)}) collective-permute-start(f32[64,1024]{1,0:T(8,128)S(1)} %fusion.19), channel_id=1, source_target_pairs={{0,2},{1,3},{2,4},{3,5},{4,6},{5,7},{6,8},{7,9},{8,10},{9,11},{10,... | collective-permute-start | bytes 786440 | tf_op jit(solution)/shard_map/ppermute | solution.py:53
  140.9 12.6 %collective-permute-start.25 = (f32[64,1024]{1,0:T(8,128)S(1)}, f32[64,1024]{1,0:T(8,128)S(1)}, u32[]{:S(2)}, u32[]{:S(2)}) collective-permute-start(f32[64,1024]{1,0:T(8,128)S(1)} %fusion.50), channel_id=1, source_target_pairs={{0,0},{1,16},{2,2},{3,18},{4,4},{5,20},{6,6},{7,22},{8,8},{9,24},{... | collective-permute-start | bytes 786440 | tf_op jit(solution)/shard_map/ppermute | solution.py:53
  148.1 8.0 %copy-start.8 = (f32[64,1024]{1,0:T(8,128)S(1)}, f32[64,1024]{1,0:T(8,128)}, u32[]{:S(2)}) copy-start(f32[64,1024]{1,0:T(8,128)} %param.9) | copy-start | bytes 786436
  148.1 8.0 %collective-permute-start.22 = (f32[64,1024]{1,0:T(8,128)S(1)}, f32[64,1024]{1,0:T(8,128)S(1)}, u32[]{:S(2)}, u32[]{:S(2)}) collective-permute-start(f32[64,1024]{1,0:T(8,128)S(1)} %fusion.10), channel_id=1, source_target_pairs={{0,2},{1,18},{2,4},{3,20},{4,6},{5,22},{6,8},{7,24},{8,10},{9,26},... | collective-permute-start | bytes 786440 | tf_op jit(solution)/shard_map/ppermute | solution.py:53
  (4 other events, 12.2 us)
